TPU v7x, 32 devices: a whole 2x2x4 slice. The times are simulated.
32 devices in a mesh: seq: 16 (over z, y, x), tp: 2 (over core).
Axes of the slice: x: 2, y: 2, z: 4, core: 2. Of those that a mesh axis runs over, the one named last changes fastest.
Arguments:
- tokens: float32 [4096, 768], P('seq'), may hold values from -6 to 6
- cotangent: float32 [4096, 768], P('seq'), may hold values from -6 to 6
- norm1_gain: float32 [768], replicated, may hold values from 0.5 to 1.5
- norm1_bias: float32 [768], replicated, may hold values from -1.75 to 1.75
- query_weight: float32 [768, 768], P(None, 'tp'), may hold values from -0.21875 to 0.21875
- query_bias: float32 [768], P('tp'), may hold values from -1.75 to 1.75
- key_weight: float32 [768, 768], P(None, 'tp'), may hold values from -0.21875 to 0.21875
- key_bias: float32 [768], P('tp'), may hold values from -1.75 to 1.75
- value_weight: float32 [768, 768], P(None, 'tp'), may hold values from -0.21875 to 0.21875
- value_bias: float32 [768], P('tp'), may hold values from -1.75 to 1.75
- shift_kernel: float32 [4, 768], P(None, 'tp'), may hold values from -3 to 3
- log_step: float32 [768], P('tp'), as said below
- state_rate: float32 [64, 768], P(None, 'tp'), may hold values from 1 to 64
- state_out: float32 [64, 768], P(None, 'tp'), may hold values from -0.75 to 0.75
- skip_gain: float32 [768], P('tp'), may hold values from -4 to 4
- out_weight: float32 [768, 768], P('tp'), may hold values from -0.21875 to 0.21875
- out_bias: float32 [768], replicated, may hold values from -1.75 to 1.75
- norm2_gain: float32 [768], replicated, may hold values from 0.5 to 1.5
- norm2_bias: float32 [768], replicated, may hold values from -1.75 to 1.75
- up_weight: float32 [768, 3072], P(None, 'tp'), may hold values from -0.21875 to 0.21875
- up_bias: float32 [3072], P('tp'), may hold values from -1.75 to 1.75
- down_weight: float32 [3072, 768], P('tp'), may hold values from -0.109375 to 0.109375
- down_bias: float32 [768], replicated, may hold values from -1.75 to 1.75
Outputs:
- block_out: float32 [4096, 768], P('seq')
- input_grad: float32 [4096, 768], P('seq')
- grad_norm1_gain: float32 [768], replicated
- grad_norm1_bias: float32 [768], replicated
- grad_query_weight: float32 [768, 768], P(None, 'tp')
- grad_query_bias: float32 [768], P('tp')
- grad_key_weight: float32 [768, 768], P(None, 'tp')
- grad_key_bias: float32 [768], P('tp')
- grad_value_weight: float32 [768, 768], P(None, 'tp')
- grad_value_bias: float32 [768], P('tp')
- grad_shift_kernel: float32 [4, 768], P(None, 'tp')
- grad_log_step: float32 [768], P('tp')
- grad_state_rate: float32 [64, 768], P(None, 'tp')
- grad_state_out: float32 [64, 768], P(None, 'tp')
- grad_skip_gain: float32 [768], P('tp')
- grad_out_weight: float32 [768, 768], P('tp')
- grad_out_bias: float32 [768], replicated
- grad_norm2_gain: float32 [768], replicated
- grad_norm2_bias: float32 [768], replicated
- grad_up_weight: float32 [768, 3072], P(None, 'tp')
- grad_up_bias: float32 [3072], P('tp')
- grad_down_weight: float32 [3072, 768], P('tp')
- grad_down_bias: float32 [768], replicated
Inputs may be any that keep to these rules, and one draw needn't show every extreme that they name: `log_step`: uniform between log(0.05 / 2048) and log(0.005).
All inputs are finite; a program needn't handle non-finite values.
Results may differ from a plain program's by a relative error of at most 0.0003.
Values sent between devices are 32-bit elements; how exact they have to be, the bound alone decides.
A program may use at most 256 MiB of HBM per device.

v0:
```python
import jax
import jax.numpy as jnp
from jax import lax
from jax.sharding import PartitionSpec as P

SHIFT = 4
STRETCH = 128
SEQS = 2


EPSILON = 1e-05
HIGHEST = lax.Precision.HIGHEST


def from_behind(value, axis, steps):
    count = lax.axis_size(axis)
    first, last = (max(0, -steps), min(count, count - steps))
    return lax.ppermute(value, axis, [(source, source + steps) for source in range(first, last)])


def prefix(array, axis, combine, identity, reverse):
    peers, index = (lax.axis_size(axis), lax.axis_index(axis))
    everything = jax.tree.map(lambda part: lax.all_gather(part, axis), array)
    start = jax.tree.map(
        lambda part, zero: jnp.broadcast_to(jnp.asarray(zero, part.dtype), part.shape),
        array,
        identity,
    )

    def lap(k, before):
        at = peers - 1 - k if reverse else k
        reached = at > index if reverse else at < index
        new = combine(before, jax.tree.map(lambda part: part[at], everything))
        return jax.tree.map(lambda a, b: jnp.where(reached, a, b), new, before)

    return lax.fori_loop(0, peers, lap, start)


def matmul(left, right):
    return jnp.dot(left, right, precision=HIGHEST, preferred_element_type=jnp.float32)


def matmul_tn(left, right):
    return lax.dot_general(
        left, right, (((0,), (0,)), ((), ())), precision=HIGHEST, preferred_element_type=jnp.float32
    )


def matmul_nt(left, right):
    return lax.dot_general(
        left, right, (((1,), (1,)), ((), ())), precision=HIGHEST, preferred_element_type=jnp.float32
    )


def layer_norm(values, gain, bias):
    centered = values - jnp.mean(values, axis=-1, keepdims=True)
    spread = jnp.mean(centered * centered, axis=-1, keepdims=True)
    return centered * lax.rsqrt(spread + EPSILON) * gain + bias


def decay_terms(log_step, state_rate):
    decay_rate = jnp.exp(log_step)[None, :] * state_rate
    return (jnp.exp(-decay_rate), jnp.sqrt(-jnp.expm1(-2.0 * decay_rate)))


def stretch_states(inputs, in_coef, decay_rate, carry_state, lower_ones):
    length = inputs.shape[0]
    places = jnp.arange(length).astype(jnp.float32)[:, None, None]
    growth = jnp.exp(decay_rate[None] * places)
    scaled = growth * (in_coef[None] * inputs[:, None, :])
    summed = matmul(lower_ones, scaled.reshape(length, -1)).reshape(scaled.shape)
    return summed / growth + jnp.exp(-decay_rate[None] * (places + 1.0)) * carry_state[None]


def combine_states(earlier, later):
    return (earlier[0] * later[1] + later[0], earlier[1] * later[1])


def on_device(
    tokens,
    cotangent,
    norm1_gain,
    norm1_bias,
    query_weight,
    query_bias,
    key_weight,
    key_bias,
    value_weight,
    value_bias,
    shift_kernel,
    log_step,
    state_rate,
    state_out,
    skip_gain,
    out_weight,
    out_bias,
    norm2_gain,
    norm2_bias,
    up_weight,
    up_bias,
    down_weight,
    down_bias,
):
    tok_rows = tokens.shape[0]
    width_local = query_weight.shape[1]
    block_count = tok_rows // STRETCH
    seq_index = lax.axis_index("seq")
    seq_span = lax.axis_size("seq") // SEQS
    seq_place = seq_index % seq_span
    keep_first = (seq_place != 0).astype(jnp.float32)
    keep_last = (seq_place != seq_span - 1).astype(jnp.float32)
    lower_ones = jnp.tril(jnp.ones((STRETCH, STRETCH), jnp.float32))
    zero_state = jnp.zeros_like(state_rate)
    one_state = jnp.ones_like(state_rate)
    normed, norm1_pull = jax.vjp(layer_norm, tokens, norm1_gain, norm1_bias)
    queries = matmul(normed, query_weight) + query_bias
    key_rows = matmul(normed, key_weight) + key_bias
    value_rows = matmul(normed, value_weight) + value_bias
    tail_rows = from_behind(key_rows[tok_rows - (SHIFT - 1) :], "seq", 1) * keep_first
    extended = jnp.concatenate([tail_rows, key_rows], axis=0)
    shifted = jnp.zeros_like(key_rows)
    for offset in range(SHIFT):
        shifted = (
            shifted
            + shift_kernel[offset] * extended[SHIFT - 1 - offset : SHIFT - 1 - offset + tok_rows]
        )
    mixed = shifted * value_rows
    decay_rate = jnp.exp(log_step)[None, :] * state_rate
    decay_factor, in_coef = decay_terms(log_step, state_rate)
    device_decay = jnp.exp(-decay_rate * tok_rows)
    blocks = mixed.reshape(block_count, STRETCH, width_local)

    def end_step(state_carry, token_block):
        states = stretch_states(token_block, in_coef, decay_rate, state_carry, lower_ones)
        return (states[-1], None)

    local_end, _ = lax.scan(end_step, zero_state, blocks)
    incoming = prefix(
        (local_end * keep_last, device_decay * keep_last),
        "seq",
        combine_states,
        (zero_state, one_state),
        False,
    )[0]

    def out_step(state_carry, token_block):
        states = stretch_states(token_block, in_coef, decay_rate, state_carry, lower_ones)
        return (states[-1], (jnp.sum(states * state_out[None], axis=1), state_carry))

    _, (ssm_blocks, block_starts) = lax.scan(out_step, incoming, blocks)
    ssm_out = ssm_blocks.reshape(tok_rows, width_local) + skip_gain * mixed
    gated = queries * ssm_out
    merged = lax.psum(matmul(gated, out_weight), "tp") + out_bias
    middle = tokens + merged
    normed2, norm2_pull = jax.vjp(layer_norm, middle, norm2_gain, norm2_bias)
    activated, gelu_pull = jax.vjp(jax.nn.gelu, matmul(normed2, up_weight) + up_bias)
    block_out = middle + lax.psum(matmul(activated, down_weight), "tp") + down_bias
    grad_down_weight = matmul_tn(activated, cotangent)
    grad_down_bias = jnp.sum(cotangent, axis=0)
    (grad_pre,) = gelu_pull(matmul_nt(cotangent, down_weight))
    grad_up_weight = matmul_tn(normed2, grad_pre)
    grad_up_bias = jnp.sum(grad_pre, axis=0)
    grad_normed2 = lax.psum(matmul_nt(grad_pre, up_weight), "tp")
    grad_mid_norm, grad_norm2_gain, grad_norm2_bias = norm2_pull(grad_normed2)
    grad_middle = cotangent + grad_mid_norm
    grad_out_bias = jnp.sum(grad_middle, axis=0)
    grad_out_weight = matmul_tn(gated, grad_middle)
    grad_gated = matmul_nt(grad_middle, out_weight)
    grad_queries = grad_gated * ssm_out
    grad_ssm = grad_gated * queries
    grad_skip_gain = jnp.sum(grad_ssm * mixed, axis=0)
    grad_blocks = grad_ssm.reshape(block_count, STRETCH, width_local)
    reversed_grads = grad_blocks[:, ::-1]

    def adjoint_end(state_carry, grad_block):
        states = stretch_states(grad_block, state_out, decay_rate, state_carry, lower_ones)
        return (states[-1], None)

    local_first, _ = lax.scan(adjoint_end, zero_state, reversed_grads, reverse=True)
    incoming_adjoint = prefix(
        (local_first * keep_first, device_decay * keep_first),
        "seq",
        combine_states,
        (zero_state, one_state),
        True,
    )[0]

    def adjoint_step(state_carry, pieces):
        grad_reversed, grad_block, token_block, start_state = pieces
        adjoint = stretch_states(grad_reversed, state_out, decay_rate, state_carry, lower_ones)[
            ::-1
        ]
        states = stretch_states(token_block, in_coef, decay_rate, start_state, lower_ones)
        previous = jnp.concatenate([start_state[None], states[:-1]], axis=0)
        grad_mixed_block = jnp.sum(adjoint * in_coef[None], axis=1)
        decay_part = jnp.sum(adjoint * previous, axis=0)
        coef_part = jnp.sum(adjoint * token_block[:, None, :], axis=0)
        out_part = jnp.sum(grad_block[:, None, :] * states, axis=0)
        return (adjoint[0], (grad_mixed_block, decay_part, coef_part, out_part))

    _, (grad_mixed_blocks, decay_parts, coef_parts, out_parts) = lax.scan(
        adjoint_step,
        incoming_adjoint,
        (reversed_grads, grad_blocks, blocks, block_starts),
        reverse=True,
    )
    grad_mixed = grad_mixed_blocks.reshape(tok_rows, width_local) + skip_gain * grad_ssm
    grad_state_out = jnp.sum(out_parts, axis=0)
    _, decay_pull = jax.vjp(decay_terms, log_step, state_rate)
    grad_log_step, grad_state_rate = decay_pull(
        (jnp.sum(decay_parts, axis=0), jnp.sum(coef_parts, axis=0))
    )
    grad_shifted = grad_mixed * value_rows
    grad_values = grad_mixed * shifted
    head_rows = from_behind(grad_shifted[: SHIFT - 1], "seq", -1) * keep_last
    grad_extended = jnp.concatenate([grad_shifted, head_rows], axis=0)
    grad_keys = jnp.zeros_like(grad_shifted)
    for offset in range(SHIFT):
        grad_keys = grad_keys + shift_kernel[offset] * grad_extended[offset : offset + tok_rows]
    grad_shift_kernel = jnp.stack(
        [
            jnp.sum(
                grad_shifted * extended[SHIFT - 1 - offset : SHIFT - 1 - offset + tok_rows], axis=0
            )
            for offset in range(SHIFT)
        ]
    )
    grad_query_weight = matmul_tn(normed, grad_queries)
    grad_key_weight = matmul_tn(normed, grad_keys)
    grad_value_weight = matmul_tn(normed, grad_values)
    grad_query_bias = jnp.sum(grad_queries, axis=0)
    grad_key_bias = jnp.sum(grad_keys, axis=0)
    grad_value_bias = jnp.sum(grad_values, axis=0)
    local_normed = (
        matmul_nt(grad_queries, query_weight)
        + matmul_nt(grad_keys, key_weight)
        + matmul_nt(grad_values, value_weight)
    )
    grad_normed = lax.psum(local_normed, "tp")
    grad_in_norm, grad_norm1_gain, grad_norm1_bias = norm1_pull(grad_normed)
    input_grad = grad_middle + grad_in_norm
    (
        grad_norm1_gain,
        grad_norm1_bias,
        grad_query_weight,
        grad_query_bias,
        grad_key_weight,
        grad_key_bias,
        grad_value_weight,
        grad_value_bias,
        grad_shift_kernel,
        grad_log_step,
        grad_state_rate,
        grad_state_out,
        grad_skip_gain,
        grad_out_weight,
        grad_out_bias,
        grad_norm2_gain,
        grad_norm2_bias,
        grad_up_weight,
        grad_up_bias,
        grad_down_weight,
        grad_down_bias,
    ) = lax.psum(
        (
            grad_norm1_gain,
            grad_norm1_bias,
            grad_query_weight,
            grad_query_bias,
            grad_key_weight,
            grad_key_bias,
            grad_value_weight,
            grad_value_bias,
            grad_shift_kernel,
            grad_log_step,
            grad_state_rate,
            grad_state_out,
            grad_skip_gain,
            grad_out_weight,
            grad_out_bias,
            grad_norm2_gain,
            grad_norm2_bias,
            grad_up_weight,
            grad_up_bias,
            grad_down_weight,
            grad_down_bias,
        ),
        "seq",
    )
    return (
        block_out,
        input_grad,
        grad_norm1_gain,
        grad_norm1_bias,
        grad_query_weight,
        grad_query_bias,
        grad_key_weight,
        grad_key_bias,
        grad_value_weight,
        grad_value_bias,
        grad_shift_kernel,
        grad_log_step,
        grad_state_rate,
        grad_state_out,
        grad_skip_gain,
        grad_out_weight,
        grad_out_bias,
        grad_norm2_gain,
        grad_norm2_bias,
        grad_up_weight,
        grad_up_bias,
        grad_down_weight,
        grad_down_bias,
    )


def solution(mesh):
    return jax.shard_map(
        on_device,
        mesh=mesh,
        in_specs=(
            P("seq", None),
            P("seq", None),
            P(),
            P(),
            P(None, "tp"),
            P("tp"),
            P(None, "tp"),
            P("tp"),
            P(None, "tp"),
            P("tp"),
            P(None, "tp"),
            P("tp"),
            P(None, "tp"),
            P(None, "tp"),
            P("tp"),
            P("tp", None),
            P(),
            P(),
            P(),
            P(None, "tp"),
            P("tp"),
            P("tp", None),
            P(),
        ),
        out_specs=(
            P("seq", None),
            P("seq", None),
            P(),
            P(),
            P(None, "tp"),
            P("tp"),
            P(None, "tp"),
            P("tp"),
            P(None, "tp"),
            P("tp"),
            P(None, "tp"),
            P("tp"),
            P(None, "tp"),
            P(None, "tp"),
            P("tp"),
            P("tp", None),
            P(),
            P(),
            P(),
            P(None, "tp"),
            P("tp"),
            P("tp", None),
            P(),
        ),
        check_vma=False,
    )
```

profile of v0, /device:TPU:0, one launch (start us, length us, event | category | flops | bytes accessed | tf_op | source)
XLA Modules:
  0.0 1595.1 jit_solution(15828086580409039355)
XLA Ops:
  25.1 157.1 %while.103 = (s32[]{:T(128)}, f32[64,384]{1,0:T(8,128)S(1)}, f32[64,384]{1,0:T(8,128)S(1)}, f32[64,384]{1,0:T(8,128)}, f32[2,128,384]{2,1,0:T(8,128)S(1)}, /*ind...) while((s32[]{:T(128)}, f32[64,384]{1,0:T(8,128)S(1)}, ...), condition=%wide.wide.region_3.4_spmd.clone, body=%wide.wide.region_2.3_spmd.clone.sunk | while | flops 4841431040 | bytes 64784000 | solution.py:137
  31.9 18.9 %copy.99 = f32[16,8,64,384]{3,1,2,0:T(8,128)} copy(f32[16,8,64,384]{3,2,1,0:T(8,128)} %bitcast.267) | data formatting | bytes 25165824 | tf_op jit(solution)/shard_map/while
  50.8 24.8 %fusion.204 = f32[24576,128]{1,0:T(8,128)} fusion(f32[128,24576]{1,0:T(8,128)} %bitcast.260, f32[24576]{0:T(1024)S(1)} %get-tuple-element.1739, f32[128]{0:T(128)S(1)} %iota_convert_fusion.12, f32[24576]{0:T(1024)S(1)} %get-tuple-element.1740), kind=kOutput, calls=%fused_computation.4.clone.clone.1 | convolution fusion | flops 4841308160 | bytes 25362944 | tf_op jit(solution)/shard_map/while/body/eval_jaxpr/dot_general | solution.py:40
  122.4 24.8 %fusion.204 = f32[24576,128]{1,0:T(8,128)} fusion(f32[128,24576]{1,0:T(8,128)} %bitcast.260, f32[24576]{0:T(1024)S(1)} %get-tuple-element.1739, f32[128]{0:T(128)S(1)} %iota_convert_fusion.12, f32[24576]{0:T(1024)S(1)} %get-tuple-element.1740), kind=kOutput, calls=%fused_computation.4.clone.clone.1 | convolution fusion | flops 4841308160 | bytes 25362944 | tf_op jit(solution)/shard_map/while/body/eval_jaxpr/dot_general | solution.py:40
  183.9 59.1 %all-gather.11.cloned.1.call-done = f32[1024,384]{1,0:T(8,128)} async-done(((f32[64,384]{1,0:T(8,128)}), f32[1024,384]{1,0:T(8,128)}) %all-gather.11.cloned.1.call-update) | async-done | bytes 1572880 | tf_op jit(solution)/shard_map/all_gather | solution.py:23
  261.0 145.7 %while.104 = (s32[]{:T(128)}, f32[64,384]{1,0:T(8,128)S(1)}, f32[2,128,384]{2,1,0:T(8,128)}, f32[2,64,384]{2,1,0:T(8,128)}, f32[64,384]{1,0:T(8,128)S(1)}, /*ind...) while((s32[]{:T(128)}, f32[64,384]{1,0:T(8,128)S(1)}, ...), condition=%wide.wide.region_8.9_spmd.clone, body=%wide.wide.region_6.8_spmd.clone.sunk | while | flops 4863279616 | bytes 115411592 | solution.py:150
  286.0 24.8 %fusion.207 = f32[24576,128]{1,0:T(8,128)} fusion(f32[128,24576]{1,0:T(8,128)} %bitcast.264, f32[24576]{0:T(1024)S(1)} %get-tuple-element.1796, f32[128]{0:T(128)S(1)} %iota_convert_fusion.13, f32[24576]{0:T(1024)S(1)} %get-tuple-element.1797), kind=kOutput, calls=%fused_computation.24.clone.clone.1 | convolution fusion | flops 4841308160 | bytes 25362944 | tf_op jit(solution)/shard_map/while/body/eval_jaxpr/dot_general | solution.py:40
  358.6 24.8 %fusion.207 = f32[24576,128]{1,0:T(8,128)} fusion(f32[128,24576]{1,0:T(8,128)} %bitcast.264, f32[24576]{0:T(1024)S(1)} %get-tuple-element.1796, f32[128]{0:T(128)S(1)} %iota_convert_fusion.13, f32[24576]{0:T(1024)S(1)} %get-tuple-element.1797), kind=kOutput, calls=%fused_computation.24.clone.clone.1 | convolution fusion | flops 4841308160 | bytes 25362944 | tf_op jit(solution)/shard_map/while/body/eval_jaxpr/dot_general | solution.py:40
  451.8 19.9 %all-reduce.10.cloned.1.call-done = f32[256,768]{1,0:T(8,128)} async-done(((f32[256,768]{1,0:T(8,128)}), f32[256,768]{1,0:T(8,128)}) %all-reduce.10.cloned.1.call-update) | async-done | bytes 786448 | tf_op jit(solution)/shard_map/psum | solution.py:163
  482.4 144.2 %while.105 = (s32[]{:T(128)}, f32[64,384]{1,0:T(8,128)S(1)}, f32[64,384]{1,0:T(8,128)S(1)}, f32[64,384]{1,0:T(8,128)}, f32[2,128,384]{1,2,0:T(8,128)S(1)}, /*ind...) while((s32[]{:T(128)}, f32[64,384]{1,0:T(8,128)S(1)}, ...), condition=%wide.wide.region_17.18_spmd.clone, body=%wide.wide.region_16.17_spmd.clone.sunk | while | flops 4841431040 | bytes 65177220 | solution.py:179
  489.3 18.9 %copy.104 = f32[16,8,64,384]{3,1,2,0:T(8,128)} copy(f32[16,8,64,384]{3,2,1,0:T(8,128)} %bitcast.269) | data formatting | bytes 25165824 | tf_op jit(solution)/shard_map/while
  508.2 24.8 %fusion.210 = f32[24576,128]{1,0:T(8,128)} fusion(f32[128,24576]{1,0:T(8,128)} %bitcast.262, f32[24576]{0:T(1024)S(1)} %get-tuple-element.1823, f32[128]{0:T(128)S(1)} %iota_convert_fusion.14, f32[24576]{0:T(1024)S(1)} %get-tuple-element.1824), kind=kOutput, calls=%fused_computation.44.clone.clone.1 | convolution fusion | flops 4841308160 | bytes 25362944 | tf_op jit(solution)/shard_map/while/body/eval_jaxpr/dot_general | solution.py:40
  580.0 24.8 %fusion.210 = f32[24576,128]{1,0:T(8,128)} fusion(f32[128,24576]{1,0:T(8,128)} %bitcast.262, f32[24576]{0:T(1024)S(1)} %get-tuple-element.1823, f32[128]{0:T(128)S(1)} %iota_convert_fusion.14, f32[24576]{0:T(1024)S(1)} %get-tuple-element.1824), kind=kOutput, calls=%fused_computation.44.clone.clone.1 | convolution fusion | flops 4841308160 | bytes 25362944 | tf_op jit(solution)/shard_map/while/body/eval_jaxpr/dot_general | solution.py:40
  653.0 33.5 %all-gather.15.cloned.1.call-done = f32[1024,384]{1,0:T(8,128)} async-done(((f32[64,384]{1,0:T(8,128)}), f32[1024,384]{1,0:T(8,128)}) %all-gather.15.cloned.1.call-update) | async-done | bytes 1572880 | tf_op jit(solution)/shard_map/all_gather | solution.py:23
  686.5 26.3 %while.102 = (s32[]{:T(128)}, f32[64,384]{1,0:T(8,128)}, s32[]{:T(128)}, f32[16,64,384]{2,1,0:T(8,128)}, f32[16,64,384]{2,1,0:T(8,128)}, /*index=5*/s32[]{:T(128)}, s32[]{:T(128)}, s32[]{:T(128)}, s32[]{:T(128)}) while((s32[]{:T(128)}, f32[64,384]{1,0:T(8,128)}, s32[]{:T(128)}, f32[16,64,384]{2,1,0:T(8,128)}, ...), condition=%wide.region_19.20_spmd.clone, body=%wide.region_18.19_spmd.clone.sunk | while | flops 98312 | bytes 393387 | solution.py:36
  715.6 398.4 %while.106 = (s32[]{:T(128)}, f32[64,384]{1,0:T(8,128)}, f32[2,128,384]{2,1,0:T(8,128)}, f32[2,64,384]{2,1,0:T(8,128)}, f32[2,64,384]{2,1,0:T(8,128)}, /*index=5...) while((s32[]{:T(128)}, f32[64,384]{1,0:T(8,128)}, ...), condition=%wide.wide.region_25.26_spmd.clone.clone, body=%wide.wide.region_20.25_spmd.clone.clone.sunk | while | flops 9748480000 | bytes 264441808 | solution.py:201
  723.7 35.9 %fusion.214 = f32[128,24576]{0,1:T(8,128)S(1)} fusion(f32[128,384]{0,1:T(8,128)S(1)} %copy.107, f32[24576]{0:T(1024)} %get-tuple-element.1908, f32[128]{0:T(128)S(1)} %iota_convert_fusion.15, f32[24576]{0:T(1024)S(1)} %get-tuple-element.1906), kind=kLoop, calls=%fused_computation.69.clone.clone.1 | loop fusion | flops 9437184 | bytes 12976640 | tf_op jit(solution)/shard_map/while/body/eval_jaxpr/mul | solution.py:70
  759.7 72.9 %fusion.215 = (f32[24576]{0:T(1024)S(1)}, f32[128,24576]{0,1:T(8,128)S(1)}, f32[24576,128]{1,0:T(8,128)}) fusion(f32[24576]{0:T(1024)S(1)} %mul.1967, f32[128]{0:T(128)S(1)} %broadcast_add_fusion.15, f32[24576]{0:T(1024)S(1)} %copy-done.26, f32[128,384]{0,1:T(8,128)S(1)} %get-tuple-element.1704, f32[128]{0:T(128)S(1)} %iota_convert_fusion.15, ...), kind=kOutput, calls=%fused_computation.65.clone.1.clone.1 | convolution fusion | flops 4860157952 | bytes 38634496 | tf_op jit(solution)/shard_map/while/body/eval_jaxpr/dot_general | solution.py:40
  885.8 19.3 %fusion.218 = f32[127,64,384]{2,1,0:T(8,128)} fusion(f32[128,64,384]{2,1,0:T(8,128)} %get-tuple-element.1708, f32[127,64,384]{2,1,0:T(8,128)} %copy.109, f32[128,64,384]{2,1,0:T(8,128)} %get-tuple-element.1710, f32[64,384]{1,0:T(8,128)S(1)} %fusion.217), kind=kLoop, calls=%fused_computation.79.clone.clone.1 | loop fusion | flops 9363456 | bytes 50036736 | tf_op jit(solution)/shard_map/while/body/eval_jaxpr/add | solution.py:72
  922.8 35.9 %fusion.214 = f32[128,24576]{0,1:T(8,128)S(1)} fusion(f32[128,384]{0,1:T(8,128)S(1)} %copy.107, f32[24576]{0:T(1024)} %get-tuple-element.1908, f32[128]{0:T(128)S(1)} %iota_convert_fusion.15, f32[24576]{0:T(1024)S(1)} %get-tuple-element.1906), kind=kLoop, calls=%fused_computation.69.clone.clone.1 | loop fusion | flops 9437184 | bytes 12976640 | tf_op jit(solution)/shard_map/while/body/eval_jaxpr/mul | solution.py:70
  958.8 72.9 %fusion.215 = (f32[24576]{0:T(1024)S(1)}, f32[128,24576]{0,1:T(8,128)S(1)}, f32[24576,128]{1,0:T(8,128)}) fusion(f32[24576]{0:T(1024)S(1)} %mul.1967, f32[128]{0:T(128)S(1)} %broadcast_add_fusion.15, f32[24576]{0:T(1024)S(1)} %copy-done.26, f32[128,384]{0,1:T(8,128)S(1)} %get-tuple-element.1704, f32[128]{0:T(128)S(1)} %iota_convert_fusion.15, ...), kind=kOutput, calls=%fused_computation.65.clone.1.clone.1 | convolution fusion | flops 4860157952 | bytes 38634496 | tf_op jit(solution)/shard_map/while/body/eval_jaxpr/dot_general | solution.py:40
  1084.9 19.3 %fusion.218 = f32[127,64,384]{2,1,0:T(8,128)} fusion(f32[128,64,384]{2,1,0:T(8,128)} %get-tuple-element.1708, f32[127,64,384]{2,1,0:T(8,128)} %copy.109, f32[128,64,384]{2,1,0:T(8,128)} %get-tuple-element.1710, f32[64,384]{1,0:T(8,128)S(1)} %fusion.217), kind=kLoop, calls=%fused_computation.79.clone.clone.1 | loop fusion | flops 9363456 | bytes 50036736 | tf_op jit(solution)/shard_map/while/body/eval_jaxpr/add | solution.py:72
  1158.2 80.9 %all-reduce = (f32[768]{0:T(1024)}, f32[768]{0:T(1024)}, f32[384]{0:T(512)}, f32[384]{0:T(512)}, f32[384]{0:T(512)}, /*index=5*/f32[4,384]{1,0:T(4,128)}, f32[38...) all-reduce(f32[768]{0:T(1024)} %get-tuple-element.1030, ...), channel_id=1, replica_groups=mesh['seq'=16,'tp'=2] {'seq'}, use_global_device_ids=true, to_apply=%region_30.31 | all-reduce | flops 9600 | bytes 76800 | tf_op jit(solution)/shard_map/psum | solution.py:264
  1243.4 330.3 %all-reduce.12.cloned.1.call-done = (f32[768,384]{1,0:T(8,128)}, f32[768,384]{1,0:T(8,128)}, f32[768,384]{1,0:T(8,128)}, f32[64,384]{1,0:T(8,128)}, f32[64,384]{...) async-done(((f32[768,384]{1,0:T(8,128)}, f32[768,384]{1,0:T(8,128)}, f32[768,384]{1,0:T(8,128)}, f32[64,384]{1,0:T(8,128)}, ...) | async-done | bytes 14352400 | tf_op jit(solution)/shard_map/psum | solution.py:264
  (449 shorter events, 613.8 us)
Async XLA Ops:
  7.3 176.6 %all-gather.9.cloned.1.call-start = ((), (), s32[]{:S(2)}) async-start(), calls=%async_computation.2 | async-start | bytes 1671168 | tf_op jit(solution)/shard_map/all_gather | solution.py:23
  10.4 232.6 %all-gather.11.cloned.1.call-start = ((), (), s32[]{:S(2)}) async-start(), calls=%async_computation.3 | async-start | bytes 1671168 | tf_op jit(solution)/shard_map/all_gather | solution.py:23
  16.3 6.2 collective-permute-start
  25.0 235.9 %copy-start.20 = (f32[64,384]{1,0:T(8,128)S(1)}, f32[64,384]{1,0:T(8,128)}, u32[]{:S(2)}) copy-start(f32[64,384]{1,0:T(8,128)} %param.48) | copy-start | bytes 294916
  182.9 250.3 %all-reduce.8.cloned.1.call-start = ((), (), s32[]{:S(2)}) async-start(), calls=%async_computation | async-start | bytes 1572864 | tf_op jit(solution)/shard_map/psum | solution.py:153
  261.0 145.8 %copy-start.2 = (f32[256,768]{1,0:T(8,128)S(1)}, f32[256,768]{1,0:T(8,128)}, u32[]{:S(2)}) copy-start(f32[256,768]{1,0:T(8,128)} %param.35) | copy-start | bytes 2359300
  261.0 145.8 %copy-start.45 = (f32[768]{0:T(1024)S(1)}, f32[768]{0:T(1024)}, u32[]{:S(2)}) copy-start(f32[768]{0:T(1024)} %param.37) | copy-start | bytes 9220
  261.0 145.8 %copy-start.48 = (f32[768]{0:T(1024)S(1)}, f32[768]{0:T(1024)}, u32[]{:S(2)}) copy-start(f32[768]{0:T(1024)} %param.38) | copy-start | bytes 9220
  261.0 145.8 %copy-start.51 = (f32[256]{0:T(256)S(1)}, f32[256]{0:T(256)}, u32[]{:S(2)}) copy-start(f32[256]{0:T(256)} %copy-done.50) | copy-start | bytes 3076
  261.0 145.8 %copy-start.56 = (f32[256]{0:T(256)S(1)}, f32[256]{0:T(256)}, u32[]{:S(2)}) copy-start(f32[256]{0:T(256)} %copy-done.55) | copy-start | bytes 3076
  261.0 145.8 %copy-start.64 = (f32[384]{0:T(512)S(1)}, f32[384]{0:T(512)}, u32[]{:S(2)}) copy-start(f32[384]{0:T(512)} %param.49) | copy-start | bytes 4612
  261.0 145.8 %copy-start.84 = (f32[384]{0:T(512)S(1)}, f32[384]{0:T(512)}, u32[]{:S(2)}) copy-start(f32[384]{0:T(512)} %param.40) | copy-start | bytes 4612
  415.1 56.6 %all-reduce.10.cloned.1.call-start = ((), (), s32[]{:S(2)}) async-start(), calls=%async_computation.1 | async-start | bytes 1572864 | tf_op jit(solution)/shard_map/psum | solution.py:163
  451.1 201.9 %all-gather.13.cloned.1.call-start = ((), (), s32[]{:S(2)}) async-start(), calls=%async_computation.4 | async-start | bytes 1671168 | tf_op jit(solution)/shard_map/all_gather | solution.py:23
  451.7 234.8 %all-gather.15.cloned.1.call-start = ((), (), s32[]{:S(2)}) async-start(), calls=%async_computation.5 | async-start | bytes 1671168 | tf_op jit(solution)/shard_map/all_gather | solution.py:23
  482.2 147.4 %copy-start.13 = (f32[64,384]{1,0:T(8,128)S(1)}, f32[64,384]{1,0:T(8,128)}, u32[]{:S(2)}) copy-start(f32[64,384]{1,0:T(8,128)} %get-tuple-element.1973) | copy-start | bytes 294916
  627.3 528.8 %all-reduce.14.cloned.1.call-start = ((), (), s32[]{:S(2)}) async-start(), calls=%async_computation.7 | async-start | bytes 3145728 | tf_op jit(solution)/shard_map/psum | solution.py:157
  645.2 70.4 %copy-start.5 = (f32[2,128,384]{2,1,0:T(8,128)S(1)}, f32[2,128,384]{2,1,0:T(8,128)}, u32[]{:S(2)}) copy-start(f32[2,128,384]{2,1,0:T(8,128)} %copy-done.4) | copy-start | bytes 1179652
  645.2 70.4 %copy-start.14 = (f32[64,384]{1,0:T(8,128)S(1)}, f32[64,384]{1,0:T(8,128)}, u32[]{:S(2)}) copy-start(f32[64,384]{1,0:T(8,128)} %get-tuple-element.1973) | copy-start | bytes 294916
  645.2 70.4 %copy-start.16 = (f32[2,128,384]{1,2,0:T(8,128)S(1)}, f32[2,128,384]{1,2,0:T(8,128)}, u32[]{:S(2)}) copy-start(f32[2,128,384]{1,2,0:T(8,128)} %copy-done.15) | copy-start | bytes 1179652
  715.6 398.4 %copy-start.59 = (f32[3,384]{1,0:T(4,128)S(1)}, f32[3,384]{1,0:T(4,128)}, u32[]{:S(2)}) copy-start(f32[3,384]{1,0:T(4,128)} %copy-done.58) | copy-start | bytes 13828
  1116.8 5.5 collective-permute-start.1
  1127.1 446.6 %all-reduce.12.cloned.1.call-start = ((), (), s32[]{:S(2)}) async-start(), calls=%async_computation.6 | async-start | bytes 28704768 | tf_op jit(solution)/shard_map/psum | solution.py:264
  1150.5 89.3 %copy-start.8 = (f32[256,768]{1,0:T(8,128)S(1)}, f32[256,768]{1,0:T(8,128)}, u32[]{:S(2)}) copy-start(f32[256,768]{1,0:T(8,128)} %copy-done.6) | copy-start | bytes 2359300
  (84 other events, 966.2 us)
Sparse Core Ops, SparseCore 0:
  11.4 60.5 all-gather.8
  183.1 59.8 all-gather.10
  415.2 17.9 all-reduce.7
  451.3 20.3 all-reduce.9
  474.9 59.0 all-gather.12
  627.5 59.0 all-gather.14
  1127.2 20.1 all-reduce.13
  1156.7 416.9 all-reduce.11
where the time goes:
time: 1600 us
  waiting for transfers between devices  456 us (28%)
  matrix products  400 us (25%)
  local copies, waits for them, and re-layouts  369 us (23%)
  other arithmetic  251 us (16%)
  blocking collectives  80.9 us (5%)
  loops' own time  16 us (1%)
    dot_general x16, matrix products, matmul(): jnp.dot(left, right, precision=HIGHEST, preferred_element_type=jnp.float32)  350 us
    psum x1, waiting for transfers between devices, on_device(): lax.psum((grad_norm1_gain, grad_norm1_bias, grad_query_weight, grad_query...  330 us
    while x52, local copies, waits for them, and re-layouts  188 us
    all_gather x4, waiting for transfers between devices, prefix(): everything = jax.tree.map(lambda part: lax.all_gather(part, axis), array)  92.6 us
    psum x1, blocking collectives, on_device(): lax.psum((grad_norm1_gain, grad_norm1_bias, grad_query_weight, grad_query...  80.9 us
    mul x2, other arithmetic, stretch_states(): scaled = growth * (in_coef[None] * inputs[:, None, :])  71.9 us
    reshape x4, local copies, waits for them, and re-layouts, stretch_states(): matmul(lower_ones, scaled.reshape(length, -1)).reshape(scaled.shape)  51.3 us
    select_n x32, other arithmetic, lap(): return jax.tree.map(lambda a, b: jnp.where(reached, a, b), new, before)  42.5 us
  transfers between devices with their start and end apart: 10, of which 7 were waited for; matrix products, arithmetic and copies ran while one was open for 24% of the time, Pallas kernels for 0%

commit v1 on v0

v1 whole, which is shorter than its diff:
```python
import functools

import jax
import jax.numpy as jnp
from jax import lax
from jax.experimental import pallas as pl
from jax.experimental.pallas import tpu as pltpu
from jax.sharding import PartitionSpec as P

SHIFT = 4
SEQS = 2
STATE = 64
LANES = 128
CHUNK = 32

EPSILON = 1e-05
F32 = jnp.float32
PRECISION = lax.Precision.HIGH


def shape(*dims):
    return jax.ShapeDtypeStruct(dims, F32)


def fold_states(values):
    return jnp.sum(values.reshape(STATE // 8, 8, LANES), axis=0)


def scan_kernel(mixed_ref, decay_ref, out_coef_ref, out_ref, end_ref, starts_ref, part_ref):
    decay, out_coef = decay_ref[...], out_coef_ref[...]

    def chunk(k, state):
        starts_ref[k] = state
        base = pl.multiple_of(k * CHUNK, CHUNK)
        for j in range(CHUNK):
            state = decay * state + mixed_ref[pl.ds(base + j, 1), :]
            part_ref[j] = fold_states(out_coef * state)
        out_ref[pl.ds(base, CHUNK), :] = jnp.sum(part_ref[...], axis=1)
        return state

    end_ref[...] = lax.fori_loop(0, mixed_ref.shape[0] // CHUNK, chunk, jnp.zeros_like(decay))


def carry_kernel(incoming_ref, decay_ref, out_coef_ref, local_ref, local_starts_ref, out_ref, starts_ref, part_ref):
    decay, out_coef = decay_ref[...], out_coef_ref[...]

    def chunk(k, state):
        starts_ref[k] = local_starts_ref[k] + state
        base = pl.multiple_of(k * CHUNK, CHUNK)
        for j in range(CHUNK):
            state = decay * state
            part_ref[j] = fold_states(out_coef * state)
        rows = pl.ds(base, CHUNK)
        out_ref[rows, :] = local_ref[rows, :] + jnp.sum(part_ref[...], axis=1)
        return state

    lax.fori_loop(0, local_ref.shape[0] // CHUNK, chunk, incoming_ref[...])


def adjoint_end_kernel(grad_ref, decay_ref, end_ref):
    decay = decay_ref[...]
    count = grad_ref.shape[0] // CHUNK

    def chunk(i, adjoint):
        base = pl.multiple_of((count - 1 - i) * CHUNK, CHUNK)
        for j in range(CHUNK - 1, -1, -1):
            adjoint = decay * adjoint + grad_ref[pl.ds(base + j, 1), :]
        return adjoint

    end_ref[...] = lax.fori_loop(0, count, chunk, jnp.zeros_like(decay))


def adjoint_kernel(
    grad_ref, mixed_ref, decay_ref, out_coef_ref, incoming_ref, starts_ref, out_ref, coef_ref, slope_ref, part_ref, state_ref
):
    decay = decay_ref[...]
    count = grad_ref.shape[0] // CHUNK
    coef_ref[...] = jnp.zeros_like(decay)
    slope_ref[...] = jnp.zeros_like(decay)

    def chunk(i, adjoint):
        k = count - 1 - i
        base = pl.multiple_of(k * CHUNK, CHUNK)
        state = starts_ref[k]
        for j in range(CHUNK):
            state_ref[j] = state
            state = decay * state + mixed_ref[pl.ds(base + j, 1), :]
        out_coef = out_coef_ref[...]
        coef, slope = coef_ref[...], slope_ref[...]
        for j in range(CHUNK - 1, -1, -1):
            adjoint = decay * adjoint + grad_ref[pl.ds(base + j, 1), :]
            part_ref[j] = fold_states(out_coef * adjoint)
            coef = coef + adjoint * mixed_ref[pl.ds(base + j, 1), :]
            slope = slope + adjoint * state_ref[j]
        coef_ref[...] = coef
        slope_ref[...] = slope
        out_ref[pl.ds(base, CHUNK), :] = jnp.sum(part_ref[...], axis=1)
        return adjoint

    lax.fori_loop(0, count, chunk, incoming_ref[...])


def state_call(kernel, args, outs, scratch, name):
    def spec(dims):
        lead = len(dims) - 1
        return pl.BlockSpec(tuple(dims[:-1]) + (LANES,), lambda i: (0,) * lead + (i,))

    return pl.pallas_call(
        kernel,
        grid=(args[0].shape[-1] // LANES,),
        in_specs=[spec(a.shape) for a in args],
        out_specs=[spec(o.shape) for o in outs],
        out_shape=outs,
        scratch_shapes=[pltpu.VMEM(dims, F32) for dims in scratch],
        compiler_params=pltpu.CompilerParams(vmem_limit_bytes=32 * 2**20),
        name=name,
    )(*args)


def within_sequence(value, shift, span):
    count = lax.axis_size("seq")
    pairs = [(i, i + shift) for i in range(count) if 0 <= i % span + shift < span]
    return lax.ppermute(value, "seq", pairs)


def carried(ends, device_decay, span, direction):
    total = None
    arrived = [within_sequence(ends, direction * k, span) for k in range(1, span)]
    for value in reversed(arrived):
        total = value if total is None else total * device_decay + value
    return jnp.zeros_like(ends) if total is None else total


def over_cores(value):
    count = lax.axis_size("tp")
    total = value
    for shift in range(1, count):
        total = total + lax.ppermute(value, "tp", [(i, (i + shift) % count) for i in range(count)])
    return total


def matmul(left, right):
    return jnp.dot(left, right, precision=PRECISION, preferred_element_type=F32)


def matmul_tn(left, right):
    return lax.dot_general(left, right, (((0,), (0,)), ((), ())), precision=PRECISION, preferred_element_type=F32)


def matmul_nt(left, right):
    return lax.dot_general(left, right, (((1,), (1,)), ((), ())), precision=PRECISION, preferred_element_type=F32)


def layer_norm(values, gain, bias):
    centered = values - jnp.mean(values, axis=-1, keepdims=True)
    spread = jnp.mean(centered * centered, axis=-1, keepdims=True)
    return centered * lax.rsqrt(spread + EPSILON) * gain + bias


def decay_terms(log_step, state_rate):
    decay_rate = jnp.exp(log_step)[None, :] * state_rate
    return (jnp.exp(-decay_rate), jnp.sqrt(-jnp.expm1(-2.0 * decay_rate)))


def on_device(
    tokens,
    cotangent,
    norm1_gain,
    norm1_bias,
    query_weight,
    query_bias,
    key_weight,
    key_bias,
    value_weight,
    value_bias,
    shift_kernel,
    log_step,
    state_rate,
    state_out,
    skip_gain,
    out_weight,
    out_bias,
    norm2_gain,
    norm2_bias,
    up_weight,
    up_bias,
    down_weight,
    down_bias,
):
    tok_rows = tokens.shape[0]
    width_local = query_weight.shape[1]
    span = lax.axis_size("seq") // SEQS
    chunks = tok_rows // CHUNK
    normed, norm1_pull = jax.vjp(layer_norm, tokens, norm1_gain, norm1_bias)
    queries = matmul(normed, query_weight) + query_bias
    key_rows = matmul(normed, key_weight) + key_bias
    value_rows = matmul(normed, value_weight) + value_bias
    tail_rows = within_sequence(key_rows[tok_rows - (SHIFT - 1) :], 1, span)
    extended = jnp.concatenate([tail_rows, key_rows], axis=0)
    behind = [extended[SHIFT - 1 - j : SHIFT - 1 - j + tok_rows] for j in range(SHIFT)]
    shifted = sum(shift_kernel[j] * behind[j] for j in range(SHIFT))
    mixed = shifted * value_rows
    decay_rate = jnp.exp(log_step)[None, :] * state_rate
    (decay_factor, in_coef), decay_pull = jax.vjp(decay_terms, log_step, state_rate)
    device_decay = jnp.exp(-decay_rate * tok_rows)
    out_coef = in_coef * state_out
    tok_shape, state_shape = shape(tok_rows, width_local), shape(STATE, width_local)
    starts_shape = shape(chunks, STATE, width_local)
    part_scratch = (CHUNK, 8, LANES)
    local_out, local_end, local_starts = state_call(
        scan_kernel,
        (mixed, decay_factor, out_coef),
        [tok_shape, state_shape, starts_shape],
        [part_scratch],
        "ssm_scan",
    )
    incoming = carried(local_end, device_decay, span, 1)
    scanned, starts = state_call(
        carry_kernel,
        (incoming, decay_factor, out_coef, local_out, local_starts),
        [tok_shape, starts_shape],
        [part_scratch],
        "ssm_carry",
    )
    ssm_out = scanned + skip_gain * mixed
    gated = queries * ssm_out
    middle = tokens + over_cores(matmul(gated, out_weight)) + out_bias
    normed2, norm2_pull = jax.vjp(layer_norm, middle, norm2_gain, norm2_bias)
    activated, gelu_pull = jax.vjp(jax.nn.gelu, matmul(normed2, up_weight) + up_bias)
    (grad_pre,) = gelu_pull(matmul_nt(cotangent, down_weight))
    grad_normed2 = over_cores(matmul_nt(grad_pre, up_weight))
    block_out = middle + over_cores(matmul(activated, down_weight)) + down_bias
    grad_down_weight = matmul_tn(activated, cotangent)
    grad_down_bias = jnp.sum(cotangent, axis=0)
    grad_up_weight = matmul_tn(normed2, grad_pre)
    grad_up_bias = jnp.sum(grad_pre, axis=0)
    grad_mid_norm, grad_norm2_gain, grad_norm2_bias = norm2_pull(grad_normed2)
    grad_middle = cotangent + grad_mid_norm
    grad_out_bias = jnp.sum(grad_middle, axis=0)
    grad_gated = matmul_nt(grad_middle, out_weight)
    grad_queries = grad_gated * ssm_out
    grad_ssm = grad_gated * queries
    grad_skip_gain = jnp.sum(grad_ssm * mixed, axis=0)
    (local_first,) = state_call(
        adjoint_end_kernel, (grad_ssm, decay_factor), [state_shape], [], "ssm_adjoint_end"
    )
    incoming_adjoint = carried(local_first, device_decay, span, -1)
    scanned_grad, coef_sum, slope_sum = state_call(
        adjoint_kernel,
        (grad_ssm, mixed, decay_factor, out_coef, incoming_adjoint, starts),
        [tok_shape, state_shape, state_shape],
        [part_scratch, (CHUNK, STATE, LANES)],
        "ssm_adjoint",
    )
    grad_mixed = scanned_grad + skip_gain * grad_ssm
    grad_state_out = in_coef * coef_sum
    grad_log_step, grad_state_rate = decay_pull((out_coef * slope_sum, state_out * coef_sum))
    grad_shifted = grad_mixed * value_rows
    grad_values = grad_mixed * shifted
    head_rows = within_sequence(grad_shifted[: SHIFT - 1], -1, span)
    grad_extended = jnp.concatenate([grad_shifted, head_rows], axis=0)
    grad_keys = sum(shift_kernel[j] * grad_extended[j : j + tok_rows] for j in range(SHIFT))
    grad_shift_kernel = jnp.stack([jnp.sum(grad_shifted * behind[j], axis=0) for j in range(SHIFT)])
    grad_out_weight = matmul_tn(gated, grad_middle)
    grad_query_weight = matmul_tn(normed, grad_queries)
    grad_key_weight = matmul_tn(normed, grad_keys)
    grad_value_weight = matmul_tn(normed, grad_values)
    grad_query_bias = jnp.sum(grad_queries, axis=0)
    grad_key_bias = jnp.sum(grad_keys, axis=0)
    grad_value_bias = jnp.sum(grad_values, axis=0)
    local_normed = (
        matmul_nt(grad_queries, query_weight)
        + matmul_nt(grad_keys, key_weight)
        + matmul_nt(grad_values, value_weight)
    )
    grad_normed = over_cores(local_normed)
    grad_in_norm, grad_norm1_gain, grad_norm1_bias = norm1_pull(grad_normed)
    input_grad = grad_middle + grad_in_norm
    (
        grad_norm1_gain,
        grad_norm1_bias,
        grad_query_weight,
        grad_query_bias,
        grad_key_weight,
        grad_key_bias,
        grad_value_weight,
        grad_value_bias,
        grad_shift_kernel,
        grad_log_step,
        grad_state_rate,
        grad_state_out,
        grad_skip_gain,
        grad_out_weight,
        grad_out_bias,
        grad_norm2_gain,
        grad_norm2_bias,
        grad_up_weight,
        grad_up_bias,
        grad_down_weight,
        grad_down_bias,
    ) = lax.psum(
        (
            grad_norm1_gain,
            grad_norm1_bias,
            grad_query_weight,
            grad_query_bias,
            grad_key_weight,
            grad_key_bias,
            grad_value_weight,
            grad_value_bias,
            grad_shift_kernel,
            grad_log_step,
            grad_state_rate,
            grad_state_out,
            grad_skip_gain,
            grad_out_weight,
            grad_out_bias,
            grad_norm2_gain,
            grad_norm2_bias,
            grad_up_weight,
            grad_up_bias,
            grad_down_weight,
            grad_down_bias,
        ),
        "seq",
    )
    return (
        block_out,
        input_grad,
        grad_norm1_gain,
        grad_norm1_bias,
        grad_query_weight,
        grad_query_bias,
        grad_key_weight,
        grad_key_bias,
        grad_value_weight,
        grad_value_bias,
        grad_shift_kernel,
        grad_log_step,
        grad_state_rate,
        grad_state_out,
        grad_skip_gain,
        grad_out_weight,
        grad_out_bias,
        grad_norm2_gain,
        grad_norm2_bias,
        grad_up_weight,
        grad_up_bias,
        grad_down_weight,
        grad_down_bias,
    )


def solution(mesh):
    return jax.shard_map(
        on_device,
        mesh=mesh,
        in_specs=(
            P("seq", None),
            P("seq", None),
            P(),
            P(),
            P(None, "tp"),
            P("tp"),
            P(None, "tp"),
            P("tp"),
            P(None, "tp"),
            P("tp"),
            P(None, "tp"),
            P("tp"),
            P(None, "tp"),
            P(None, "tp"),
            P("tp"),
            P("tp", None),
            P(),
            P(),
            P(),
            P(None, "tp"),
            P("tp"),
            P("tp", None),
            P(),
        ),
        out_specs=(
            P("seq", None),
            P("seq", None),
            P(),
            P(),
            P(None, "tp"),
            P("tp"),
            P(None, "tp"),
            P("tp"),
            P(None, "tp"),
            P("tp"),
            P(None, "tp"),
            P("tp"),
            P(None, "tp"),
            P(None, "tp"),
            P("tp"),
            P("tp", None),
            P(),
            P(),
            P(),
            P(None, "tp"),
            P("tp"),
            P("tp", None),
            P(),
        ),
        check_vma=False,
    )
```

time: 1600 us -> 558 us (0.35)
  matrix products: 400 us -> 37.8 us
  local copies, waits for them, and re-layouts: 369 us -> 15.2 us
  other arithmetic: 251 us -> 13.2 us
  waiting for transfers between devices: 456 us -> 343 us
  starting transfers between devices: 6.66 us -> 34.4 us
  Pallas kernels: 0 us -> 19.5 us
  loops' own time: 16 us -> 0 us
    dot_general x28 -> x18, matrix products: 400 us -> 37.8 us  [the longest x6 16.6 us: matmul_tn(): lax.dot_general(left, right, (((0,), (0,)), ((), ())), precision=PRECISIO...]
    while x52 -> x0, local copies, waits for them, and re-layouts: 188 us -> none
    all_gather x4 -> x0, waiting for transfers between devices: 92.6 us -> none  [prefix(): everything = jax.tree.map(lambda part: lax.all_gather(part, axis), array)]
    mul x7 -> x1, other arithmetic: 74.7 us -> 0.08 us  [on_device(): out_coef = in_coef * state_out]
    slice x15 -> x3, local copies, waits for them, and re-layouts: 54.3 us -> 0.04 us  [the longest x1 0.03 us: on_device(): shifted = sum((shift_kernel[j] * behind[j] for j in range(SHIFT)))]
    reshape x5 -> x0, local copies, waits for them, and re-layouts: 51.5 us -> none  [the longest x4 51.3 us: stretch_states(): matmul(lower_ones, scaled.reshape(length, -1)).reshape(scaled.shape)]
    select_n x32 -> x0, other arithmetic: 42.5 us -> none  [lap(): return jax.tree.map(lambda a, b: jnp.where(reached, a, b), new, before)]
    add x10 -> x2, other arithmetic: 38.5 us -> 0.13 us  [carried(): total = value if total is None else total * device_decay + value]
  transfers between devices with their start and end apart: 10 -> 21, of which waited for: 7 -> 11; matrix products, arithmetic and copies ran while one was open for 24% -> 5% of each run, Pallas kernels for 0% -> 0%
where the time goes in v1:
time: 558 us; the launch traced here: 557 us
  waiting for transfers between devices  343 us (61%)
  blocking collectives  78.8 us (14%)
  matrix products  37.8 us (7%)
  starting transfers between devices  34.4 us (6%)
  Pallas kernels  19.5 us (3%)
  local copies, waits for them, and re-layouts  15.2 us (3%)
  between operations  14.9 us (3%)
  other arithmetic  13.2 us (2%)
    psum x1, waiting for transfers between devices, on_device(): lax.psum((grad_norm1_gain, grad_norm1_bias, grad_query_weight, grad_query...  328 us
    psum x1, blocking collectives, on_device(): lax.psum((grad_norm1_gain, grad_norm1_bias, grad_query_weight, grad_query...  78.8 us
    ppermute x16, starting transfers between devices, within_sequence(): return lax.ppermute(value, 'seq', pairs)  33.6 us
    pallas_call x4, Pallas kernels, state_call(): pl.pallas_call(kernel, grid=(args[0].shape[-1] // LANES,), in_specs=[spec...  19.5 us
    dot_general x6, matrix products, matmul_tn(): lax.dot_general(left, right, (((0,), (0,)), ((), ())), precision=PRECISIO...  16.6 us
    unnamed x96, local copies, waits for them, and re-layouts  15.1 us
    ppermute x16, waiting for transfers between devices, within_sequence(): return lax.ppermute(value, 'seq', pairs)  14.7 us
    dot_general x6, matrix products, matmul(): return jnp.dot(left, right, precision=PRECISION, preferred_element_type=F32)  11.5 us
  transfers between devices with their start and end apart: 21, of which 11 were waited for; matrix products, arithmetic and copies ran while one was open for 5% of the time, Pallas kernels for 0%

profile of v1, /device:TPU:0, one launch (start us, length us, event | category | flops | bytes accessed | tf_op | source)
XLA Modules:
  0.0 557.2 jit_solution(6916110254255999698)
XLA Ops:
  10.8 2.3 convolution_add_fusion.4
  13.1 4.8 collective-permute-start
  20.3 4.3 ssm_scan.1
  24.6 4.3 collective-permute-start.7
  28.9 3.4 collective-permute-start.6
  32.3 5.3 collective-permute-start.5
  46.1 3.7 ssm_carry.1
  52.1 2.2 fusion.63
  55.0 3.7 fusion.48
  58.8 2.2 fusion.64
  61.0 2.9 fusion.7
  64.5 4.4 fusion.8
  68.9 4.7 fusion.6
  93.3 3.0 collective-permute-done.13
  96.3 3.4 collective-permute-done.12
  99.7 2.0 collective-permute-done.11
  101.8 9.7 %ssm_adjoint.1 = (f32[256,384]{1,0:T(8,128)S(1)}, f32[64,384]{1,0:T(8,128)S(1)}, f32[64,384]{1,0:T(8,128)S(1)}) custom-call(f32[256,384]{1,0:T(8,128)S(1)} %get-tuple-element.81.grad_ref, f32[256,384]{1,0:T(8,128)S(1)} %get-tuple-element.97.mixed_ref, f32[64,384]{1,0:T(8,128)S(1)} %get-tuple-element.110.decay_ref, ...), custom_call_target="tpu_custom_call" | custom-call | tf_op jit(solution)/shard_map/ssm_adjoint/pallas_call | solution.py:108
  119.4 2.0 fusion.46
  121.4 2.2 fusion.65
  128.7 78.8 %all-reduce = (f32[768]{0:T(1024)}, f32[768]{0:T(1024)}, f32[384]{0:T(512)}, f32[384]{0:T(512)}, f32[384]{0:T(512)}, /*index=5*/f32[4,384]{1,0:T(4,128)}, f32[38...) all-reduce(f32[768]{0:T(1024)} %get-tuple-element.41, ...), channel_id=1, replica_groups=mesh['seq'=16,'tp'=2] {'seq'}, use_global_device_ids=true, to_apply=%region_9.0 | all-reduce | flops 9600 | bytes 76800 | tf_op jit(solution)/shard_map/psum | solution.py:301
  209.6 327.7 %all-reduce.4.cloned.1.call-done = (f32[768,384]{1,0:T(8,128)}, f32[768,384]{1,0:T(8,128)}, f32[768,384]{1,0:T(8,128)}, f32[64,384]{1,0:T(8,128)}, f32[64,384]{1...) async-done(((f32[768,384]{1,0:T(8,128)}, f32[768,384]{1,0:T(8,128)}, f32[768,384]{1,0:T(8,128)}, f32[64,384]{1,0:T(8,128)}, ...) | async-done | bytes 14352400 | tf_op jit(solution)/shard_map/psum | solution.py:301
  537.3 2.5 copy.54
  544.7 2.4 copy.60
  548.2 2.2 copy.61
  (176 shorter events, 58.3 us)
Async XLA Ops:
  7.2 530.0 %all-reduce.4.cloned.1.call-start = ((), (), s32[]{:S(2)}) async-start(), calls=%async_computation | async-start | bytes 28704768 | tf_op jit(solution)/shard_map/psum | solution.py:301
  10.8 41.3 %slice-start = ((s8[4718592]{0:T(1024)(128)(4,1)}), s8[4194304]{0:T(1024)(128)(4,1)S(1)}, s32[]{:S(2)}) async-start(s8[4718592]{0:T(1024)(128)(4,1)} %bitcast.26), calls=%async_computation.1 | async-start | bytes 8388608
  13.1 6.2 %collective-permute-start = (f32[3,384]{1,0:T(4,128)S(1)}, f32[3,384]{1,0:T(4,128)S(1)}, u32[]{:S(2)}, u32[]{:S(2)}) collective-permute-start(f32[3,384]{1,0:T(4,128)S(1)} %slice.52), channel_id=1, source_target_pairs={{0,2},{2,4},{4,6},{6,8},{8,10},{10,12},{12,14},{16,18},{18,20},{20... | collective-permute-start | bytes 13832 | tf_op jit(solution)/shard_map/ppermute | solution.py:123
  20.2 29.6 %copy-start.6 = (f32[768,384]{1,0:T(8,128)S(1)}, f32[768,384]{1,0:T(8,128)}, u32[]{:S(2)}) copy-start(f32[768,384]{1,0:T(8,128)} %param.27) | copy-start | bytes 3538948
  20.2 29.6 %copy-start.21 = (f32[384]{0:T(512)S(1)}, f32[384]{0:T(512)}, u32[]{:S(2)}) copy-start(f32[384]{0:T(512)} %param.37) | copy-start | bytes 4612
  24.6 15.6 %collective-permute-start.7 = (f32[64,384]{1,0:T(8,128)S(1)}, f32[64,384]{1,0:T(8,128)S(1)}, u32[]{:S(2)}, u32[]{:S(2)}) collective-permute-start(f32[64,384]{1,0:T(8,128)S(1)} %get-tuple-element.31), channel_id=1, source_target_pairs={{0,2},{2,4},{4,6},{6,8},{8,10},{10,12},{12,14},{16,18},{18,20},{20... | collective-permute-start | bytes 294920 | tf_op jit(solution)/shard_map/ppermute | solution.py:123
  28.9 12.6 %collective-permute-start.6 = (f32[64,384]{1,0:T(8,128)S(1)}, f32[64,384]{1,0:T(8,128)S(1)}, u32[]{:S(2)}, u32[]{:S(2)}) collective-permute-start(f32[64,384]{1,0:T(8,128)S(1)} %get-tuple-element.31), channel_id=1, source_target_pairs={{0,4},{2,6},{4,8},{6,10},{8,12},{10,14},{16,20},{18,22},{20,24},{2... | collective-permute-start | bytes 294920 | tf_op jit(solution)/shard_map/ppermute | solution.py:123
  32.3 10.5 %collective-permute-start.5 = (f32[64,384]{1,0:T(8,128)S(1)}, f32[64,384]{1,0:T(8,128)S(1)}, u32[]{:S(2)}, u32[]{:S(2)}) collective-permute-start(f32[64,384]{1,0:T(8,128)S(1)} %get-tuple-element.31), channel_id=1, source_target_pairs={{0,6},{2,8},{4,10},{6,12},{8,14},{16,22},{18,24},{20,26},{22,28},{... | collective-permute-start | bytes 294920 | tf_op jit(solution)/shard_map/ppermute | solution.py:123
  37.6 5.2 collective-permute-start.4
  38.9 5.0 collective-permute-start.3
  40.2 4.8 collective-permute-start.2
  41.5 4.5 collective-permute-start.1
  52.0 2.4 collective-permute-start.8
  63.9 10.6 %collective-permute-start.9 = (f32[256,768]{1,0:T(8,128)S(1)}, f32[256,768]{1,0:T(8,128)S(1)}, u32[]{:S(2)}, u32[]{:S(2)}) collective-permute-start(f32[256,768]{1,0:T(8,128)S(1)} %fusion.7), channel_id=1, source_target_pairs={{0,1},{1,0},{2,3},{3,2},{4,5},{5,4},{6,7},{7,6},{8,9},{9,8},{10,11... | collective-permute-start | bytes 2359304 | tf_op jit(solution)/shard_map/ppermute | solution.py:138
  64.4 9.1 %collective-permute-start.10 = (f32[256,768]{1,0:T(8,128)S(1)}, f32[256,768]{1,0:T(8,128)S(1)}, u32[]{:S(2)}, u32[]{:S(2)}) collective-permute-start(f32[256,768]{1,0:T(8,128)S(1)} %fusion.64), channel_id=1, source_target_pairs={{0,1},{1,0},{2,3},{3,2},{4,5},{5,4},{6,7},{7,6},{8,9},{9,8},{10,11... | collective-permute-start | bytes 2359304 | tf_op jit(solution)/shard_map/ppermute | solution.py:138
  79.7 8.4 %collective-permute-start.17 = (f32[64,384]{1,0:T(8,128)S(1)}, f32[64,384]{1,0:T(8,128)S(1)}, u32[]{:S(2)}, u32[]{:S(2)}) collective-permute-start(f32[64,384]{1,0:T(8,128)S(1)} %ssm_adjoint_end.1), channel_id=1, source_target_pairs={{2,0},{4,2},{6,4},{8,6},{10,8},{12,10},{14,12},{18,16},{20,18},{22... | collective-permute-start | bytes 294920 | tf_op jit(solution)/shard_map/ppermute | solution.py:123
  81.0 8.4 %collective-permute-start.16 = (f32[64,384]{1,0:T(8,128)S(1)}, f32[64,384]{1,0:T(8,128)S(1)}, u32[]{:S(2)}, u32[]{:S(2)}) collective-permute-start(f32[64,384]{1,0:T(8,128)S(1)} %ssm_adjoint_end.1), channel_id=1, source_target_pairs={{4,0},{6,2},{8,4},{10,6},{12,8},{14,10},{20,16},{22,18},{24,20},{2... | collective-permute-start | bytes 294920 | tf_op jit(solution)/shard_map/ppermute | solution.py:123
  82.3 10.2 %collective-permute-start.15 = (f32[64,384]{1,0:T(8,128)S(1)}, f32[64,384]{1,0:T(8,128)S(1)}, u32[]{:S(2)}, u32[]{:S(2)}) collective-permute-start(f32[64,384]{1,0:T(8,128)S(1)} %ssm_adjoint_end.1), channel_id=1, source_target_pairs={{6,0},{8,2},{10,4},{12,6},{14,8},{22,16},{24,18},{26,20},{28,22},{... | collective-permute-start | bytes 294920 | tf_op jit(solution)/shard_map/ppermute | solution.py:123
  83.6 9.6 %collective-permute-start.14 = (f32[64,384]{1,0:T(8,128)S(1)}, f32[64,384]{1,0:T(8,128)S(1)}, u32[]{:S(2)}, u32[]{:S(2)}) collective-permute-start(f32[64,384]{1,0:T(8,128)S(1)} %ssm_adjoint_end.1), channel_id=1, source_target_pairs={{8,0},{10,2},{12,4},{14,6},{24,16},{26,18},{28,20},{30,22},{9,1},{... | collective-permute-start | bytes 294920 | tf_op jit(solution)/shard_map/ppermute | solution.py:123
  84.9 11.4 %collective-permute-start.13 = (f32[64,384]{1,0:T(8,128)S(1)}, f32[64,384]{1,0:T(8,128)S(1)}, u32[]{:S(2)}, u32[]{:S(2)}) collective-permute-start(f32[64,384]{1,0:T(8,128)S(1)} %ssm_adjoint_end.1), channel_id=1, source_target_pairs={{10,0},{12,2},{14,4},{26,16},{28,18},{30,20},{11,1},{13,3},{15,5},... | collective-permute-start | bytes 294920 | tf_op jit(solution)/shard_map/ppermute | solution.py:123
  88.2 11.5 %collective-permute-start.12 = (f32[64,384]{1,0:T(8,128)S(1)}, f32[64,384]{1,0:T(8,128)S(1)}, u32[]{:S(2)}, u32[]{:S(2)}) collective-permute-start(f32[64,384]{1,0:T(8,128)S(1)} %ssm_adjoint_end.1), channel_id=1, source_target_pairs={{12,0},{14,2},{28,16},{30,18},{13,1},{15,3},{29,17},{31,19}} | collective-permute-start | bytes 294920 | tf_op jit(solution)/shard_map/ppermute | solution.py:123
  89.5 12.2 %collective-permute-start.11 = (f32[64,384]{1,0:T(8,128)S(1)}, f32[64,384]{1,0:T(8,128)S(1)}, u32[]{:S(2)}, u32[]{:S(2)}) collective-permute-start(f32[64,384]{1,0:T(8,128)S(1)} %ssm_adjoint_end.1), channel_id=1, source_target_pairs={{14,0},{30,16},{15,1},{31,17}} | collective-permute-start | bytes 294920 | tf_op jit(solution)/shard_map/ppermute | solution.py:123
  112.3 5.5 collective-permute-start.18
  125.3 2.4 collective-permute-start.19
  (41 other events, 183.4 us)
Sparse Core Ops, SparseCore 0:
  121.5 415.7 all-reduce.3

commit v2 on v1

--- a/solution.py
+++ b/solution.py
@@ -12,6 +12,8 @@
 STATE = 64
 LANES = 128
 CHUNK = 32
+PIECE_ROWS = 24
+LAG = 2
 
 EPSILON = 1e-05
 F32 = jnp.float32
@@ -137,6 +139,205 @@
     for shift in range(1, count):
         total = total + lax.ppermute(value, "tp", [(i, (i + shift) % count) for i in range(count)])
     return total
+
+
+MESH = pl.DeviceIdType.MESH
+
+
+def is_far(i):
+    return lax.rem(i, 4) == 2
+
+
+def sum_kernel(
+    length, pieces, rows, lag, own_ref, out_ref, sum_ref, got_ref, load_sem, store_sem, chain_send, chain_recv,
+    z_send, z_recv, side_send, side_recv
+):
+    me = lax.axis_index("seq")
+    place, quarter = me // 4, lax.rem(me, 4)
+    x, y = lax.rem(quarter, 2), quarter // 2
+    x_peer, y_peer = me + 1 - 2 * x, me + 2 - 4 * y
+    quarter_x, quarter_y, quarter_d = quarter + 1 - 2 * x, quarter + 2 - 4 * y, 3 - quarter
+    first = lag * (length - 1)
+    started = (place, length - 1 - place)
+    ahead = (me + 4, me - 4)
+    behind = (me - 4, me + 4)
+
+    loads = [pltpu.make_async_copy(own_ref.at[d], sum_ref.at[d], load_sem.at[d]) for d in range(2)]
+    for load in loads:
+        load.start()
+    barrier = pltpu.get_barrier_semaphore()
+
+    def greet(peer):
+        pl.semaphore_signal(barrier, inc=1, device_id={"seq": peer}, device_id_type=MESH)
+
+    greet(x_peer)
+    greet(y_peer)
+    pl.when(place > 0)(lambda: greet(me - 4))
+    pl.when(place < length - 1)(lambda: greet(me + 4))
+    pl.semaphore_wait(barrier, 2 + (place > 0).astype(jnp.int32) + (place < length - 1).astype(jnp.int32))
+    for load in loads:
+        load.wait()
+
+    def remote(source, target, send, recv, peer):
+        return pltpu.make_async_remote_copy(
+            src_ref=source,
+            dst_ref=target,
+            send_sem=send,
+            recv_sem=recv,
+            device_id={"seq": peer},
+            device_id_type=MESH,
+        )
+
+    def at(i):
+        return pl.ds(pl.multiple_of(i * rows, 8), rows)
+
+    def chain_copy(d, i):
+        return remote(
+            sum_ref.at[d, at(i)], got_ref.at[d, at(i)], chain_send.at[d, i], chain_recv.at[d, i], ahead[d]
+        )
+
+    def z_copy(d, i, k):
+        ref = out_ref.at[(quarter, quarter_x, quarter_y, quarter_d)[k], d, at(i)]
+        return remote(ref, ref, z_send.at[d, i, k], z_recv.at[d, i, k], behind[d])
+
+    def side_copy(d, i, k):
+        even = lax.rem(i, 2) == 0
+        source = (quarter, quarter, jnp.where(even, quarter_x, quarter_y))[k]
+        peer = (x_peer, y_peer, jnp.where(even, y_peer, x_peer))[k]
+        ref = out_ref.at[source, d, at(i)]
+        return remote(ref, ref, side_send.at[d, i, k], side_recv.at[d, i, k], peer)
+
+    def chain_step(d, i):
+        @pl.when(started[d] > 0)
+        def _():
+            chain_copy(d, i).wait_recv()
+            sum_ref[d, at(i)] = sum_ref[d, at(i)] + got_ref[d, at(i)]
+
+        @pl.when(started[d] < length - 1)
+        def _():
+            chain_copy(d, i).start()
+
+        @pl.when(started[d] == length - 1)
+        def _():
+            store = pltpu.make_async_copy(sum_ref.at[d, at(i)], out_ref.at[quarter, d, at(i)], store_sem.at[d, i])
+            store.start()
+            store.wait()
+
+    def kind(d, i):
+        remaining = length - 1 - started[d]
+        far = is_far(i)
+        sideways = jnp.logical_or(jnp.logical_not(far), remaining == 0)
+        onward = jnp.logical_and(far, remaining < length - 1)
+        return remaining, sideways, onward
+
+    def own_step(d, i):
+        remaining, sideways, _ = kind(d, i)
+
+        @pl.when(remaining > 0)
+        def _():
+            z_copy(d, i, 0).wait_recv()
+
+        @pl.when(remaining < length - 1)
+        def _():
+            z_copy(d, i, 0).start()
+
+        @pl.when(sideways)
+        def _():
+            side_copy(d, i, 0).start()
+            side_copy(d, i, 1).start()
+
+    def side_step(d, i):
+        _, sideways, onward = kind(d, i)
+
+        @pl.when(sideways)
+        def _():
+            side_copy(d, i, 0).wait_recv()
+            side_copy(d, i, 1).wait_recv()
+            side_copy(d, i, 2).start()
+
+        @pl.when(jnp.logical_not(sideways))
+        def _():
+            z_copy(d, i, 1).wait_recv()
+            z_copy(d, i, 2).wait_recv()
+
+        @pl.when(onward)
+        def _():
+            z_copy(d, i, 1).start()
+            z_copy(d, i, 2).start()
+
+    def last_step(d, i):
+        _, sideways, onward = kind(d, i)
+
+        @pl.when(sideways)
+        def _():
+            side_copy(d, i, 2).wait_recv()
+
+        @pl.when(jnp.logical_not(sideways))
+        def _():
+            z_copy(d, i, 3).wait_recv()
+
+        @pl.when(onward)
+        def _():
+            z_copy(d, i, 3).start()
+
+    def tick(t, _):
+        for step, late in ((last_step, first + 2 * lag), (side_step, first + lag), (chain_step, 0), (own_step, first)):
+            for d in range(2):
+                passed = started[d] if step is chain_step else length - 1 - started[d]
+                i = t - late - lag * passed
+                pl.when(jnp.logical_and(i >= 0, i < pieces))(functools.partial(step, d, i))
+        return 0
+
+    lax.fori_loop(0, 2 * first + 2 * lag + pieces, tick, 0)
+
+    def drain(i, _):
+        for d in range(2):
+            remaining, sideways, onward = kind(d, i)
+            pl.when(remaining > 0)(lambda: chain_copy(d, i).wait_send())
+            pl.when(remaining < length - 1)(lambda: z_copy(d, i, 0).wait_send())
+
+            @pl.when(onward)
+            def _():
+                for k in range(1, 4):
+                    z_copy(d, i, k).wait_send()
+
+            @pl.when(sideways)
+            def _():
+                for k in range(3):
+                    side_copy(d, i, k).wait_send()
+
+        return 0
+
+    lax.fori_loop(0, pieces, drain, 0)
+
+
+def summed_quarters(own, pieces, lag):
+    _, total, columns = own.shape
+    length = lax.axis_size("seq") // 4
+    sems = [(2,), (2, pieces), (2, pieces), (2, pieces), (2, pieces, 4), (2, pieces, 4), (2, pieces, 3), (2, pieces, 3)]
+    return pl.pallas_call(
+        functools.partial(sum_kernel, length, pieces, total // pieces, lag),
+        out_shape=shape(4, 2, total, columns),
+        in_specs=[pl.BlockSpec(memory_space=pl.ANY)],
+        out_specs=pl.BlockSpec(memory_space=pltpu.HBM),
+        scratch_shapes=[pltpu.VMEM((2, total, columns), F32)] * 2 + [pltpu.SemaphoreType.DMA(dims) for dims in sems],
+        compiler_params=pltpu.CompilerParams(collective_id=0, has_side_effects=True, vmem_limit_bytes=32 * 2**20),
+        cost_estimate=pl.CostEstimate(flops=total * columns * 2, bytes_accessed=total * columns * 64, transcendentals=0),
+        name="gradient_sums",
+    )(own)
+
+
+def swapped(value, bit):
+    return lax.ppermute(value, "seq", [(i, i ^ bit) for i in range(lax.axis_size("seq"))])
+
+
+def half(value, axis, which):
+    size = value.shape[axis] // 2
+    return lax.dynamic_slice_in_dim(value, which * size, size, axis)
+
+
+def halved_sum(value, bit, mine):
+    return half(value, 0, mine) + swapped(half(value, 0, 1 - mine), bit)
 
 
 def matmul(left, right):
@@ -191,6 +392,7 @@
     width_local = query_weight.shape[1]
     span = lax.axis_size("seq") // SEQS
     chunks = tok_rows // CHUNK
+    x, y = lax.axis_index("seq") % 2, lax.axis_index("seq") // 2 % 2
     normed, norm1_pull = jax.vjp(layer_norm, tokens, norm1_gain, norm1_bias)
     queries = matmul(normed, query_weight) + query_bias
     key_rows = matmul(normed, key_weight) + key_bias
@@ -230,10 +432,16 @@
     (grad_pre,) = gelu_pull(matmul_nt(cotangent, down_weight))
     grad_normed2 = over_cores(matmul_nt(grad_pre, up_weight))
     block_out = middle + over_cores(matmul(activated, down_weight)) + down_bias
-    grad_down_weight = matmul_tn(activated, cotangent)
     grad_down_bias = jnp.sum(cotangent, axis=0)
-    grad_up_weight = matmul_tn(normed2, grad_pre)
     grad_up_bias = jnp.sum(grad_pre, axis=0)
+    down_half = matmul_tn(half(activated, 1, x), cotangent) + matmul_tn(
+        swapped(half(activated, 1, 1 - x), 1), swapped(cotangent, 1)
+    )
+    up_half = matmul_tn(normed2, half(grad_pre, 1, y)) + matmul_tn(
+        swapped(normed2, 2), swapped(half(grad_pre, 1, 1 - y), 2)
+    )
+    down_quarter = halved_sum(down_half, 2, y)
+    up_quarter = halved_sum(up_half, 1, x)
     grad_mid_norm, grad_norm2_gain, grad_norm2_bias = norm2_pull(grad_normed2)
     grad_middle = cotangent + grad_mid_norm
     grad_out_bias = jnp.sum(grad_middle, axis=0)
@@ -261,10 +469,6 @@
     grad_extended = jnp.concatenate([grad_shifted, head_rows], axis=0)
     grad_keys = sum(shift_kernel[j] * grad_extended[j : j + tok_rows] for j in range(SHIFT))
     grad_shift_kernel = jnp.stack([jnp.sum(grad_shifted * behind[j], axis=0) for j in range(SHIFT)])
-    grad_out_weight = matmul_tn(gated, grad_middle)
-    grad_query_weight = matmul_tn(normed, grad_queries)
-    grad_key_weight = matmul_tn(normed, grad_keys)
-    grad_value_weight = matmul_tn(normed, grad_values)
     grad_query_bias = jnp.sum(grad_queries, axis=0)
     grad_key_bias = jnp.sum(grad_keys, axis=0)
     grad_value_bias = jnp.sum(grad_values, axis=0)
@@ -276,54 +480,84 @@
     grad_normed = over_cores(local_normed)
     grad_in_norm, grad_norm1_gain, grad_norm1_bias = norm1_pull(grad_normed)
     input_grad = grad_middle + grad_in_norm
+    query_key = matmul_tn(normed, jnp.where(x == 0, grad_queries, grad_keys)) + matmul_tn(
+        swapped(normed, 1), swapped(jnp.where(x == 0, grad_keys, grad_queries), 1)
+    )
+    value_out = matmul_tn(jnp.where(y == 0, normed, grad_middle), jnp.where(y == 0, grad_values, gated)) + matmul_tn(
+        swapped(jnp.where(y == 0, grad_middle, normed), 2), swapped(jnp.where(y == 0, gated, grad_values), 2)
+    )
+    small = (
+        grad_norm1_gain,
+        grad_norm1_bias,
+        grad_norm2_gain,
+        grad_norm2_bias,
+        grad_out_bias,
+        grad_down_bias,
+        grad_up_bias,
+        grad_query_bias,
+        grad_key_bias,
+        grad_value_bias,
+        grad_skip_gain,
+        grad_log_step,
+        grad_shift_kernel,
+        grad_state_rate,
+        grad_state_out,
+    )
+    small_rows = jnp.concatenate([part.reshape(-1, width_local) for part in small], axis=0)
+    small_count = small_rows.shape[0]
+    small_size = -(-small_count // 32) * 8
+    small_rows = jnp.pad(small_rows, ((0, 4 * small_size - small_count), (0, 0)))
+    small_quarter = halved_sum(halved_sum(small_rows, 1, x), 2, y)
+    mixer_quarter = jnp.concatenate(
+        [halved_sum(query_key, 2, y), halved_sum(value_out, 1, x), small_quarter], axis=0
+    )
+    mixer_rows = mixer_quarter.shape[0] // 2
+    feed_rows = up_quarter.shape[0]
+    piece_rows = PIECE_ROWS
+    pieces = -(-(feed_rows + -(-mixer_rows // 2)) // piece_rows)
+    spare = 2 * (pieces * piece_rows - feed_rows) - mixer_rows
+    mixer_wide = jnp.concatenate([mixer_quarter[:mixer_rows], mixer_quarter[mixer_rows:]], axis=1)
+    mixer_wide = jnp.pad(mixer_wide, ((0, spare), (0, 0)))
+    own = jnp.concatenate(
+        [jnp.stack([up_quarter, down_quarter]), mixer_wide.reshape(2, -1, mixer_wide.shape[1])], axis=1
+    )
+    sums = summed_quarters(own, pieces, LAG)
+    width = sums.shape[-1]
+    feed = sums[:, :, :feed_rows].reshape(2, 2, 2, feed_rows, width)
+    grad_up_weight = feed[:, :, 0].transpose(1, 2, 0, 3).reshape(2 * feed_rows, 2 * width)
+    grad_down_weight = feed[:, :, 1].transpose(1, 0, 2, 3).reshape(4 * feed_rows, width)
+    rest = sums[:, :, feed_rows:].reshape(4, -1, width)[:, :mixer_rows]
+    rest = jnp.concatenate([rest[..., :width_local], rest[..., width_local:]], axis=1)
+    rest = rest.reshape(2, 2, 2 * mixer_rows, width_local)
+    projection = 2 * (width // 4)
+    grad_query_weight = rest[:, 0, :projection].reshape(-1, width_local)
+    grad_key_weight = rest[:, 1, :projection].reshape(-1, width_local)
+    grad_value_weight = rest[0, :, projection : 2 * projection].reshape(-1, width_local)
+    grad_out_weight = rest[1, :, projection : 2 * projection].reshape(-1, width_local).T
+    flat = rest[:, :, 2 * projection :].transpose(1, 0, 2, 3).reshape(-1, width_local)
+    unpacked = []
+    start = 0
+    for part in small:
+        count = part.size // width_local
+        unpacked.append(flat[start : start + count].reshape(part.shape))
+        start += count
     (
         grad_norm1_gain,
         grad_norm1_bias,
-        grad_query_weight,
+        grad_norm2_gain,
+        grad_norm2_bias,
+        grad_out_bias,
+        grad_down_bias,
+        grad_up_bias,
         grad_query_bias,
-        grad_key_weight,
         grad_key_bias,
-        grad_value_weight,
         grad_value_bias,
+        grad_skip_gain,
+        grad_log_step,
         grad_shift_kernel,
-        grad_log_step,
         grad_state_rate,
         grad_state_out,
-        grad_skip_gain,
-        grad_out_weight,
-        grad_out_bias,
-        grad_norm2_gain,
-        grad_norm2_bias,
-        grad_up_weight,
-        grad_up_bias,
-        grad_down_weight,
-        grad_down_bias,
-    ) = lax.psum(
-        (
-            grad_norm1_gain,
-            grad_norm1_bias,
-            grad_query_weight,
-            grad_query_bias,
-            grad_key_weight,
-            grad_key_bias,
-            grad_value_weight,
-            grad_value_bias,
-            grad_shift_kernel,
-            grad_log_step,
-            grad_state_rate,
-            grad_state_out,
-            grad_skip_gain,
-            grad_out_weight,
-            grad_out_bias,
-            grad_norm2_gain,
-            grad_norm2_bias,
-            grad_up_weight,
-            grad_up_bias,
-            grad_down_weight,
-            grad_down_bias,
-        ),
-        "seq",
-    )
+    ) = unpacked
     return (
         block_out,
         input_grad,

time: 558 us -> 410 us (0.73)
  waiting for transfers between devices: 343 us -> 52 us
  Pallas kernels: 19.5 us -> 162 us
  blocking collectives: 78.8 us -> 0 us
  local copies, waits for them, and re-layouts: 15.2 us -> 56.3 us
  matrix products: 37.8 us -> 55.6 us
  starting transfers between devices: 34.4 us -> 51.4 us
  other arithmetic: 13.2 us -> 25.8 us
  between operations: 14.9 us -> 2.3 us
    psum x1 -> x0, waiting for transfers between devices: 328 us -> none  [on_device(): lax.psum((grad_norm1_gain, grad_norm1_bias, grad_query_weight, grad_query...]
    pallas_call x0 -> x1, Pallas kernels: none -> 143 us  [summed_quarters(): pl.pallas_call(functools.partial(sum_kernel, length, pieces, total // pie...]
    psum x1 -> x0, blocking collectives: 78.8 us -> none  [on_device(): lax.psum((grad_norm1_gain, grad_norm1_bias, grad_query_weight, grad_query...]
    ppermute x0 -> x14, waiting for transfers between devices: none -> 25.2 us  [swapped(): lax.ppermute(value, 'seq', [(i, i ^ bit) for i in range(lax.axis_size('se...]
    ppermute x0 -> x14, starting transfers between devices: none -> 17 us  [swapped(): lax.ppermute(value, 'seq', [(i, i ^ bit) for i in range(lax.axis_size('se...]
    transpose x0 -> x3, local copies, waits for them, and re-layouts: none -> 15.4 us  [the longest x2 11.8 us: on_device(): feed[:, :, 1].transpose(1, 0, 2, 3).reshape(4 * feed_rows, width)]
    reshape x0 -> x19, local copies, waits for them, and re-layouts: none -> 13.7 us  [the longest x12 9.47 us: on_device(): part.reshape(-1, width_local)]
    ppermute x16, waiting for transfers between devices: 14.7 us -> 26.7 us  [within_sequence(): return lax.ppermute(value, 'seq', pairs)]
  transfers between devices with their start and end apart: 21 -> 34, of which waited for: 11 -> 11; matrix products, arithmetic and copies ran while one was open for 5% -> 21% of each run, Pallas kernels for 0% -> 3%
where the time goes in v2:
time: 410 us; the launch traced here: 406 us
  Pallas kernels  162 us (40%)
  local copies, waits for them, and re-layouts  56.3 us (14%)
  matrix products  55.6 us (14%)
  waiting for transfers between devices  52 us (13%)
  starting transfers between devices  51.4 us (13%)
  other arithmetic  25.8 us (6%)
    pallas_call x1, Pallas kernels, summed_quarters(): pl.pallas_call(functools.partial(sum_kernel, length, pieces, total // pie...  143 us
    ppermute x16, starting transfers between devices, within_sequence(): return lax.ppermute(value, 'seq', pairs)  33.8 us
    ppermute x16, waiting for transfers between devices, within_sequence(): return lax.ppermute(value, 'seq', pairs)  26.7 us
    ppermute x14, waiting for transfers between devices, swapped(): lax.ppermute(value, 'seq', [(i, i ^ bit) for i in range(lax.axis_size('se...  25.2 us
    dot_general x8, matrix products, matmul_tn(): lax.dot_general(left, right, (((0,), (0,)), ((), ())), precision=PRECISIO...  22.2 us
    dot_general x6, matrix products, matmul(): return jnp.dot(left, right, precision=PRECISION, preferred_element_type=F32)  19.6 us
    pallas_call x4, Pallas kernels, state_call(): pl.pallas_call(kernel, grid=(args[0].shape[-1] // LANES,), in_specs=[spec...  19.5 us
    ppermute x14, starting transfers between devices, swapped(): lax.ppermute(value, 'seq', [(i, i ^ bit) for i in range(lax.axis_size('se...  17 us
  transfers between devices with their start and end apart: 34, of which 11 were waited for; matrix products, arithmetic and copies ran while one was open for 21% of the time, Pallas kernels for 3%

profile of v2, /device:TPU:0, one launch (start us, length us, event | category | flops | bytes accessed | tf_op | source)
XLA Modules:
  0.0 405.6 jit_solution(2886873810629578419)
XLA Ops:
  6.7 4.8 %collective-permute-start = (f32[3,384]{1,0:T(4,128)S(1)}, f32[3,384]{1,0:T(4,128)S(1)}, u32[]{:S(2)}, u32[]{:S(2)}) collective-permute-start(f32[3,384]{1,0:T(4,128)S(1)} %slice.169), channel_id=1, source_target_pairs={{0,2},{2,4},{4,6},{6,8},{8,10},{10,12},{12,14},{16,18},{18,20},{20... | collective-permute-start | bytes 13832 | tf_op jit(solution)/shard_map/ppermute | solution.py:125
  15.9 4.3 %ssm_scan.1 = (f32[256,384]{1,0:T(8,128)S(1)}, f32[64,384]{1,0:T(8,128)S(1)}, f32[8,64,384]{2,1,0:T(8,128)S(1)}) custom-call(f32[256,384]{1,0:T(8,128)S(1)} %get-tuple-element.81.mixed_ref, f32[64,384]{1,0:T(8,128)S(1)} %get-tuple-element.115.decay_ref, f32[64,384]{1,0:T(8,128)S(1)} %get-tuple-element.114.out_coef_ref), custom_call_target="tpu_custom_call" | custom-call | tf_op jit(solution)/shard_map/ssm_scan/pallas_call | solution.py:110
  20.2 4.2 %collective-permute-start.7 = (f32[64,384]{1,0:T(8,128)S(1)}, f32[64,384]{1,0:T(8,128)S(1)}, u32[]{:S(2)}, u32[]{:S(2)}) collective-permute-start(f32[64,384]{1,0:T(8,128)S(1)} %get-tuple-element.31), channel_id=1, source_target_pairs={{0,2},{2,4},{4,6},{6,8},{8,10},{10,12},{12,14},{16,18},{18,20},{20... | collective-permute-start | bytes 294920 | tf_op jit(solution)/shard_map/ppermute | solution.py:125
  24.4 3.4 collective-permute-start.6
  27.9 5.3 %collective-permute-start.5 = (f32[64,384]{1,0:T(8,128)S(1)}, f32[64,384]{1,0:T(8,128)S(1)}, u32[]{:S(2)}, u32[]{:S(2)}) collective-permute-start(f32[64,384]{1,0:T(8,128)S(1)} %get-tuple-element.31), channel_id=1, source_target_pairs={{0,6},{2,8},{4,10},{6,12},{8,14},{16,22},{18,24},{20,26},{22,28},{... | collective-permute-start | bytes 294920 | tf_op jit(solution)/shard_map/ppermute | solution.py:125
  41.6 3.7 ssm_carry.1
  50.7 4.7 %fusion.65 = f32[256,1536]{1,0:T(8,128)S(1)} fusion(f32[256,768]{1,0:T(8,128)} %param.24, f32[1536,768]{1,0:T(8,128)} %param.44), kind=kOutput, calls=%fused_computation.150 | convolution fusion | flops 1811939328 | bytes 7077888 | tf_op jit(solution)/shard_map/dot_general | solution.py:352
  59.1 6.4 %fusion.51 = (f32[1536]{0:T(1024)S(1)}, f32[256,1536]{1,0:T(8,128)S(1)}, f32[256,1536]{1,0:T(8,128)S(1)}, f32[256,1536]{1,0:T(8,128)S(1)}) fusion(f32[256,1536]{1,0:T(8,128)S(1)} %fusion.65, f32[1536]{0:T(1024)S(1)} %copy-done.63, f32[256,768]{1,0:T(8,128)} %multiply_add_fusion, f32[768,1536]{1,0:T(8,128)} %param.42), kind=kOutput, calls=%fused_computation.137 | convolution fusion | flops 1820588544 | bytes 11808768 | tf_op jit(solution)/shard_map/dot_general | solution.py:344
  65.6 3.1 fusion.66
  69.1 3.7 fusion.43
  78.5 3.9 fusion.12
  82.4 3.9 fusion.14
  129.8 3.7 collective-permute-done.12
  134.9 9.7 %ssm_adjoint.1 = (f32[256,384]{1,0:T(8,128)S(1)}, f32[64,384]{1,0:T(8,128)S(1)}, f32[64,384]{1,0:T(8,128)S(1)}) custom-call(f32[256,384]{1,0:T(8,128)S(1)} %get-tuple-element.62.grad_ref, f32[256,384]{1,0:T(8,128)S(1)} %get-tuple-element.81.mixed_ref, f32[64,384]{1,0:T(8,128)S(1)} %get-tuple-element.115.decay_ref, ...), custom_call_target="tpu_custom_call" | custom-call | tf_op jit(solution)/shard_map/ssm_adjoint/pallas_call | solution.py:110
  152.8 17.4 %collective-permute-done.18 = f32[3,384]{1,0:T(4,128)S(1)} collective-permute-done((f32[3,384]{1,0:T(4,128)S(1)}, f32[3,384]{1,0:T(4,128)S(1)}, u32[]{:S(2)}, u32[]{:S(2)}) %collective-permute-start.18) | collective-permute-done | bytes 4640 | tf_op jit(solution)/shard_map/ppermute | solution.py:125
  172.4 3.0 fusion.10
  178.8 2.9 collective-permute-start.27
  198.9 11.5 %collective-permute-done.33 = f32[40,384]{1,0:T(8,128)S(1)} collective-permute-done((f32[40,384]{1,0:T(8,128)S(1)}, f32[40,384]{1,0:T(8,128)S(1)}, u32[]{:S(2)}, u32[]{:S(2)}) %collective-permute-start.33) | collective-permute-done | bytes 61472 | tf_op jit(solution)/shard_map/ppermute | solution.py:331
  214.3 10.5 %collective-permute-done.28 = f32[384,384]{1,0:T(8,128)S(1)} collective-permute-done((f32[384,384]{1,0:T(8,128)S(1)}, f32[384,384]{1,0:T(8,128)S(1)}, u32[]{:S(2)}, u32[]{:S(2)}) %collective-permute-start.28) | collective-permute-done | bytes 589856 | tf_op jit(solution)/shard_map/ppermute | solution.py:331
  228.8 142.8 %gradient_sums.1 = f32[4,2,600,768]{3,2,1,0:T(8,128)S(1)} custom-call(f32[2,600,768]{2,1,0:T(8,128)S(1)} %pad_maximum_fusion.1.own_ref), custom_call_target="tpu_custom_call" | custom-call | flops 921600 | bytes 29491200 | tf_op jit(solution)/shard_map/gradient_sums/pallas_call | solution.py:318
  377.3 4.5 %slice.164 = f32[4,2,384,768]{3,2,1,0:T(8,128)} slice(f32[4,2,600,768]{3,2,1,0:T(8,128)S(1)} %gradient_sums.1), slice={[0:4], [0:2], [0:384], [0:768]} | slice | bytes 18874368 | tf_op jit(solution)/shard_map/slice | solution.py:526
  386.2 6.9 %slice_bitcast_fusion = (f32[2,2,384,768]{3,2,0,1:T(8,128)}, f32[2,384,2,768]{3,1,0,2:T(8,128)S(1)}) fusion(f32[2,2,2,384,768]{4,3,2,1,0:T(8,128)} %bitcast.62), kind=kLoop, calls=%fused_computation.1 | loop fusion | bytes 18874368 | tf_op jit(solution)/shard_map/transpose | solution.py:528
  393.1 3.6 copy.48
  399.8 4.9 %copy.49 = f32[2,2,384,768]{3,2,1,0:T(8,128)} copy(f32[2,2,384,768]{3,2,0,1:T(8,128)} %get-tuple-element.83) | data formatting | bytes 9437184 | tf_op jit(solution)/shard_map/transpose | solution.py:528
  (316 shorter events, 130.3 us)
Async XLA Ops:
  20.2 15.5 %collective-permute-start.7 = (f32[64,384]{1,0:T(8,128)S(1)}, f32[64,384]{1,0:T(8,128)S(1)}, u32[]{:S(2)}, u32[]{:S(2)}) collective-permute-start(f32[64,384]{1,0:T(8,128)S(1)} %get-tuple-element.31), channel_id=1, source_target_pairs={{0,2},{2,4},{4,6},{6,8},{8,10},{10,12},{12,14},{16,18},{18,20},{20... | collective-permute-start | bytes 294920 | tf_op jit(solution)/shard_map/ppermute | solution.py:125
  24.4 12.6 %collective-permute-start.6 = (f32[64,384]{1,0:T(8,128)S(1)}, f32[64,384]{1,0:T(8,128)S(1)}, u32[]{:S(2)}, u32[]{:S(2)}) collective-permute-start(f32[64,384]{1,0:T(8,128)S(1)} %get-tuple-element.31), channel_id=1, source_target_pairs={{0,4},{2,6},{4,8},{6,10},{8,12},{10,14},{16,20},{18,22},{20,24},{2... | collective-permute-start | bytes 294920 | tf_op jit(solution)/shard_map/ppermute | solution.py:125
  50.6 59.2 %collective-permute-start.24 = (f32[256,768]{1,0:T(8,128)}, f32[256,768]{1,0:T(8,128)}, u32[]{:S(2)}, u32[]{:S(2)}) collective-permute-start(f32[256,768]{1,0:T(8,128)} %param.24), channel_id=1, source_target_pairs={{0,2},{2,0},{4,6},{6,4},{8,10},{10,8},{12,14},{14,12},{16,18},{18,... | collective-permute-start | bytes 2359304 | tf_op jit(solution)/shard_map/ppermute | solution.py:331
  59.1 56.2 %collective-permute-start.20 = (f32[256,768]{1,0:T(8,128)}, f32[256,768]{1,0:T(8,128)}, u32[]{:S(2)}, u32[]{:S(2)}) collective-permute-start(f32[256,768]{1,0:T(8,128)} %multiply_add_fusion), channel_id=1, source_target_pairs={{0,4},{2,6},{4,0},{6,2},{8,12},{10,14},{12,8},{14,10},{16,20},{18,... | collective-permute-start | bytes 2359304 | tf_op jit(solution)/shard_map/ppermute | solution.py:331
  68.6 17.7 %collective-permute-start.10 = (f32[256,768]{1,0:T(8,128)}, f32[256,768]{1,0:T(8,128)}, u32[]{:S(2)}, u32[]{:S(2)}) collective-permute-start(f32[256,768]{1,0:T(8,128)} %fusion.66), channel_id=1, source_target_pairs={{0,1},{1,0},{2,3},{3,2},{4,5},{5,4},{6,7},{7,6},{8,9},{9,8},{10,11... | collective-permute-start | bytes 2359304 | tf_op jit(solution)/shard_map/ppermute | solution.py:140
  72.9 17.1 %collective-permute-start.9 = (f32[256,768]{1,0:T(8,128)}, f32[256,768]{1,0:T(8,128)}, u32[]{:S(2)}, u32[]{:S(2)}) collective-permute-start(f32[256,768]{1,0:T(8,128)} %fusion.43), channel_id=1, source_target_pairs={{0,1},{1,0},{2,3},{3,2},{4,5},{5,4},{6,7},{7,6},{8,9},{9,8},{10,11... | collective-permute-start | bytes 2359304 | tf_op jit(solution)/shard_map/ppermute | solution.py:140
  74.4 36.7 %collective-permute-start.23 = (f32[256,768]{1,0:T(8,128)}, f32[256,768]{1,0:T(8,128)}, u32[]{:S(2)}, u32[]{:S(2)}) collective-permute-start(f32[256,768]{1,0:T(8,128)} %constant_dynamic-slice_fusion.4), channel_id=1, source_target_pairs={{0,2},{2,0},{4,6},{6,4},{8,10},{10,8},{12,14},{14,12},{16,18},{18,... | collective-permute-start | bytes 2359304 | tf_op jit(solution)/shard_map/ppermute | solution.py:331
  86.3 30.3 %collective-permute-start.21 = (f32[256,768]{1,0:T(8,128)}, f32[256,768]{1,0:T(8,128)}, u32[]{:S(2)}, u32[]{:S(2)}) collective-permute-start(f32[256,768]{1,0:T(8,128)} %constant_dynamic-slice_fusion.6), channel_id=1, source_target_pairs={{0,4},{2,6},{4,0},{6,2},{8,12},{10,14},{12,8},{14,10},{16,20},{18,... | collective-permute-start | bytes 2359304 | tf_op jit(solution)/shard_map/ppermute | solution.py:331
  98.6 23.3 %collective-permute-start.17 = (f32[64,384]{1,0:T(8,128)S(1)}, f32[64,384]{1,0:T(8,128)S(1)}, u32[]{:S(2)}, u32[]{:S(2)}) collective-permute-start(f32[64,384]{1,0:T(8,128)S(1)} %ssm_adjoint_end.1), channel_id=1, source_target_pairs={{2,0},{4,2},{6,4},{8,6},{10,8},{12,10},{14,12},{18,16},{20,18},{22... | collective-permute-start | bytes 294920 | tf_op jit(solution)/shard_map/ppermute | solution.py:125
  109.8 13.3 %collective-permute-start.16 = (f32[64,384]{1,0:T(8,128)S(1)}, f32[64,384]{1,0:T(8,128)S(1)}, u32[]{:S(2)}, u32[]{:S(2)}) collective-permute-start(f32[64,384]{1,0:T(8,128)S(1)} %ssm_adjoint_end.1), channel_id=1, source_target_pairs={{4,0},{6,2},{8,4},{10,6},{12,8},{14,10},{20,16},{22,18},{24,20},{2... | collective-permute-start | bytes 294920 | tf_op jit(solution)/shard_map/ppermute | solution.py:125
  111.1 14.5 %collective-permute-start.15 = (f32[64,384]{1,0:T(8,128)S(1)}, f32[64,384]{1,0:T(8,128)S(1)}, u32[]{:S(2)}, u32[]{:S(2)}) collective-permute-start(f32[64,384]{1,0:T(8,128)S(1)} %ssm_adjoint_end.1), channel_id=1, source_target_pairs={{6,0},{8,2},{10,4},{12,6},{14,8},{22,16},{24,18},{26,20},{28,22},{... | collective-permute-start | bytes 294920 | tf_op jit(solution)/shard_map/ppermute | solution.py:125
  115.3 12.4 %collective-permute-start.14 = (f32[64,384]{1,0:T(8,128)S(1)}, f32[64,384]{1,0:T(8,128)S(1)}, u32[]{:S(2)}, u32[]{:S(2)}) collective-permute-start(f32[64,384]{1,0:T(8,128)S(1)} %ssm_adjoint_end.1), channel_id=1, source_target_pairs={{8,0},{10,2},{12,4},{14,6},{24,16},{26,18},{28,20},{30,22},{9,1},{... | collective-permute-start | bytes 294920 | tf_op jit(solution)/shard_map/ppermute | solution.py:125
  116.6 13.1 %collective-permute-start.13 = (f32[64,384]{1,0:T(8,128)S(1)}, f32[64,384]{1,0:T(8,128)S(1)}, u32[]{:S(2)}, u32[]{:S(2)}) collective-permute-start(f32[64,384]{1,0:T(8,128)S(1)} %ssm_adjoint_end.1), channel_id=1, source_target_pairs={{10,0},{12,2},{14,4},{26,16},{28,18},{30,20},{11,1},{13,3},{15,5},... | collective-permute-start | bytes 294920 | tf_op jit(solution)/shard_map/ppermute | solution.py:125
  123.1 11.6 %collective-permute-start.11 = (f32[64,384]{1,0:T(8,128)S(1)}, f32[64,384]{1,0:T(8,128)S(1)}, u32[]{:S(2)}, u32[]{:S(2)}) collective-permute-start(f32[64,384]{1,0:T(8,128)S(1)} %ssm_adjoint_end.1), channel_id=1, source_target_pairs={{14,0},{30,16},{15,1},{31,17}} | collective-permute-start | bytes 294920 | tf_op jit(solution)/shard_map/ppermute | solution.py:125
  125.6 64.1 %collective-permute-start.26 = (f32[256,768]{1,0:T(8,128)}, f32[256,768]{1,0:T(8,128)}, u32[]{:S(2)}, u32[]{:S(2)}) collective-permute-start(f32[256,768]{1,0:T(8,128)} %multiply_add_fusion.1), channel_id=1, source_target_pairs={{0,2},{2,0},{4,6},{6,4},{8,10},{10,8},{12,14},{14,12},{16,18},{18,... | collective-permute-start | bytes 2359304 | tf_op jit(solution)/shard_map/ppermute | solution.py:331
  127.7 97.3 %collective-permute-start.25 = (f32[384,768]{1,0:T(8,128)}, f32[384,768]{1,0:T(8,128)}, u32[]{:S(2)}, u32[]{:S(2)}) collective-permute-start(f32[384,768]{1,0:T(8,128)} %constant_dynamic-slice_fusion.3), channel_id=1, source_target_pairs={{0,4},{2,6},{4,0},{6,2},{8,12},{10,14},{12,8},{14,10},{16,20},{18,... | collective-permute-start | bytes 3538952 | tf_op jit(solution)/shard_map/ppermute | solution.py:331
  129.7 96.8 %collective-permute-start.22 = (f32[384,768]{1,0:T(8,128)}, f32[384,768]{1,0:T(8,128)}, u32[]{:S(2)}, u32[]{:S(2)}) collective-permute-start(f32[384,768]{1,0:T(8,128)} %constant_dynamic-slice_fusion.5), channel_id=1, source_target_pairs={{0,2},{2,0},{4,6},{6,4},{8,10},{10,8},{12,14},{14,12},{16,18},{18,... | collective-permute-start | bytes 3538952 | tf_op jit(solution)/shard_map/ppermute | solution.py:331
  144.9 25.3 %collective-permute-start.18 = (f32[3,384]{1,0:T(4,128)S(1)}, f32[3,384]{1,0:T(4,128)S(1)}, u32[]{:S(2)}, u32[]{:S(2)}) collective-permute-start(f32[3,384]{1,0:T(4,128)S(1)} %slice.174), channel_id=1, source_target_pairs={{2,0},{4,2},{6,4},{8,6},{10,8},{12,10},{14,12},{18,16},{20,18},{22... | collective-permute-start | bytes 13832 | tf_op jit(solution)/shard_map/ppermute | solution.py:125
  147.6 63.2 %collective-permute-start.30 = (f32[256,384]{1,0:T(8,128)}, f32[256,384]{1,0:T(8,128)}, u32[]{:S(2)}, u32[]{:S(2)}) collective-permute-start(f32[256,384]{1,0:T(8,128)} %broadcast_select_fusion.1), channel_id=1, source_target_pairs={{0,4},{2,6},{4,0},{6,2},{8,12},{10,14},{12,8},{14,10},{16,20},{18,... | collective-permute-start | bytes 1179656 | tf_op jit(solution)/shard_map/ppermute | solution.py:331
  178.8 12.7 %collective-permute-start.27 = (f32[256,384]{1,0:T(8,128)}, f32[256,384]{1,0:T(8,128)S(1)}, u32[]{:S(2)}, u32[]{:S(2)}) collective-permute-start(f32[256,384]{1,0:T(8,128)} %broadcast_select_fusion.2), channel_id=1, source_target_pairs={{0,2},{2,0},{4,6},{6,4},{8,10},{10,8},{12,14},{14,12},{16,18},{18,... | collective-permute-start | bytes 1179656 | tf_op jit(solution)/shard_map/ppermute | solution.py:331
  189.7 21.1 %collective-permute-start.29 = (f32[256,768]{1,0:T(8,128)S(1)}, f32[256,768]{1,0:T(8,128)S(1)}, u32[]{:S(2)}, u32[]{:S(2)}) collective-permute-start(f32[256,768]{1,0:T(8,128)S(1)} %get-tuple-element.98), channel_id=1, source_target_pairs={{0,4},{2,6},{4,0},{6,2},{8,12},{10,14},{12,8},{14,10},{16,20},{18,... | collective-permute-start | bytes 2359304 | tf_op jit(solution)/shard_map/ppermute | solution.py:331
  197.4 13.1 %collective-permute-start.33 = (f32[40,384]{1,0:T(8,128)S(1)}, f32[40,384]{1,0:T(8,128)S(1)}, u32[]{:S(2)}, u32[]{:S(2)}) collective-permute-start(f32[40,384]{1,0:T(8,128)S(1)} %constant_dynamic-slice_fusion), channel_id=1, source_target_pairs={{0,4},{2,6},{4,0},{6,2},{8,12},{10,14},{12,8},{14,10},{16,20},{18,... | collective-permute-start | bytes 184328 | tf_op jit(solution)/shard_map/ppermute | solution.py:331
  210.4 14.4 %collective-permute-start.28 = (f32[384,384]{1,0:T(8,128)S(1)}, f32[384,384]{1,0:T(8,128)S(1)}, u32[]{:S(2)}, u32[]{:S(2)}) collective-permute-start(f32[384,384]{1,0:T(8,128)S(1)} %constant_dynamic-slice_fusion.2), channel_id=1, source_target_pairs={{0,4},{2,6},{4,0},{6,2},{8,12},{10,14},{12,8},{14,10},{16,20},{18,... | collective-permute-start | bytes 1769480 | tf_op jit(solution)/shard_map/ppermute | solution.py:331
  212.7 15.7 %collective-permute-start.31 = (f32[384,384]{1,0:T(8,128)S(1)}, f32[384,384]{1,0:T(8,128)S(1)}, u32[]{:S(2)}, u32[]{:S(2)}) collective-permute-start(f32[384,384]{1,0:T(8,128)S(1)} %constant_dynamic-slice_fusion.1), channel_id=1, source_target_pairs={{0,2},{2,0},{4,6},{6,4},{8,10},{10,8},{12,14},{14,12},{16,18},{18,... | collective-permute-start | bytes 1769480 | tf_op jit(solution)/shard_map/ppermute | solution.py:331
  (87 other events, 663.0 us)
